TPU v7x, 128 devices: a whole 4x4x4 slice. The times are simulated.
128 devices in a mesh: seq: 64 (over z, y, x_hi, core), head: 2 (over x_lo).
Axes of the slice: x: 4 (x_hi: 2, x_lo: 2; x = x_hi * 2 + x_lo), y: 4, z: 4, core: 2. Of those that a mesh axis runs over, the one named last changes fastest.
Arguments:
- queries: bfloat16 [32768, 5120], P(('seq', 'head')), may hold values from -8 to 8
- keys: bfloat16 [32768, 1024], P(('seq', 'head')), may hold values from -8 to 8
- values: bfloat16 [32768, 1024], P(('seq', 'head')), may hold values from -6 to 6
- output_gradient: bfloat16 [32768, 5120], P(('seq', 'head')), may hold values from -6 to 6
- document_lengths: int32 [64, 16], replicated, may hold values from 1 to 377, as said below
Outputs:
- attn_out: bfloat16 [32768, 5120], P(('seq', 'head'))
- query_grad: bfloat16 [32768, 5120], P(('seq', 'head'))
- key_grad: bfloat16 [32768, 1024], P(('seq', 'head'))
- value_grad: bfloat16 [32768, 1024], P(('seq', 'head'))
Inputs may be any that keep to these rules, and one draw needn't show every extreme that they name: `document_lengths`: every entry of a row is 1 or more; a row sums to 512; its last 8 entries sum to 128, so no document crosses the start of a block's last 128 tokens.
All inputs are finite; a program needn't handle non-finite values.
Results may differ from a plain program's by a relative error of at most 0.012.
The roundings to bfloat16 on the way count: a program that leaves them out, or rounds other values in their place, can miss the bound.
Values may be sent and summed in bfloat16 or wider, within the bound.
A program may use at most 128 MiB of HBM per device.

v0:
```python
import math

import jax
import jax.numpy as jnp
from jax import lax
from jax.sharding import PartitionSpec as P

QUERY_HEAD_COUNT = 40
KEY_VALUE_HEADS = 8
HEAD_SIZE = 128


NEG = -1e30


def passed_along(block, axis, distance):
    devices = range(lax.axis_size(axis))
    route = [((i - distance) % len(devices), i) for i in devices]
    return lax.ppermute(block, axis, route)


def doc_ids(lengths_row, count):
    starts = jnp.cumsum(lengths_row) - lengths_row
    place = jnp.arange(count, dtype=jnp.int32)
    return jnp.sum((place[:, None] >= starts[None, :]).astype(jnp.int32), axis=1) - 1


def head_pass(query_head, key_head, value_head, grad_head, visible, scale):
    scores = jnp.dot(query_head, key_head.T, preferred_element_type=jnp.float32) * scale
    scores = jnp.where(visible, scores, NEG)
    top = jnp.max(scores, axis=1, keepdims=True)
    lse = top + jnp.log(jnp.sum(jnp.exp(scores - top), axis=1, keepdims=True))
    probs = jnp.where(visible, jnp.exp(scores - lse), 0.0)
    probs_bf = probs.astype(jnp.bfloat16)
    attention_output = jnp.dot(probs_bf, value_head, preferred_element_type=jnp.float32).astype(
        jnp.bfloat16
    )
    delta = jnp.sum(
        grad_head.astype(jnp.float32) * attention_output.astype(jnp.float32), axis=1, keepdims=True
    )
    dprobs = jnp.dot(grad_head, value_head.T, preferred_element_type=jnp.float32)
    dscores = (probs * (dprobs - delta)).astype(jnp.bfloat16)
    query_grad = (jnp.dot(dscores, key_head, preferred_element_type=jnp.float32) * scale).astype(
        jnp.bfloat16
    )
    key_part = jnp.dot(dscores.T, query_head, preferred_element_type=jnp.float32) * scale
    value_part = jnp.dot(probs_bf.T, grad_head, preferred_element_type=jnp.float32)
    return (attention_output, query_grad, key_part, value_part)


def attend(
    query_rows,
    key_rows,
    value_rows,
    grad_rows,
    query_doc,
    query_pos,
    key_doc,
    key_pos,
    heads,
    group_count,
):
    rows = query_rows.shape[0]
    span = key_rows.shape[0]
    width = HEAD_SIZE
    group_ratio = heads // group_count
    scale = 1.0 / math.sqrt(HEAD_SIZE)
    visible = (query_doc[:, None] == key_doc[None, :]) & (key_pos[None, :] <= query_pos[:, None])
    query_heads = query_rows.reshape(rows, heads, width).transpose(1, 0, 2)
    grad_heads = grad_rows.reshape(rows, heads, width).transpose(1, 0, 2)
    key_heads = key_rows.reshape(span, group_count, width).transpose(1, 0, 2)
    value_heads = value_rows.reshape(span, group_count, width).transpose(1, 0, 2)
    group_of = jnp.arange(heads, dtype=jnp.int32) // group_ratio

    def per_head(parts):
        return head_pass(
            parts[0], key_heads[parts[2]], value_heads[parts[2]], parts[1], visible, scale
        )

    attention_output, query_gradient, key_portion, value_portion = lax.map(
        per_head, (query_heads, grad_heads, group_of)
    )
    key_gradient = jnp.sum(key_portion.reshape(group_count, group_ratio, span, width), axis=1)
    value_gradient = jnp.sum(value_portion.reshape(group_count, group_ratio, span, width), axis=1)
    return (
        attention_output.transpose(1, 0, 2).reshape(rows, heads * width),
        query_gradient.transpose(1, 0, 2).reshape(rows, heads * width),
        key_gradient.transpose(1, 0, 2).reshape(span, group_count * width),
        value_gradient.transpose(1, 0, 2).reshape(span, group_count * width),
    )


def part_costs(lengths_row):
    squares = lengths_row * lengths_row
    middle = lengths_row.shape[0] // 2
    return (jnp.sum(squares[:middle]), jnp.sum(squares[middle:]))


def body(queries, keys, values, output_gradient, document_lengths):
    rows = queries.shape[0]
    tail_rows = rows // 2
    keep_rows = rows - tail_rows
    seq_count = lax.axis_size("seq")
    count_of_heads = lax.axis_size("head")
    span = rows * count_of_heads
    seq_at = lax.axis_index("seq")
    head_at = lax.axis_index("head")
    place = jnp.arange(span, dtype=jnp.int32)
    own_lengths = lax.dynamic_index_in_dim(document_lengths, seq_at, 0, False)
    own_ids = doc_ids(own_lengths, span)
    partner_at = (seq_at + seq_count // 2) % seq_count
    other_lengths = lax.dynamic_index_in_dim(document_lengths, partner_at, 0, False)
    own_front, own_back = part_costs(own_lengths)
    other_front, other_back = part_costs(other_lengths)
    before = jnp.maximum(own_front + own_back, other_front + other_back)
    after = jnp.maximum(own_front + other_back, other_front + own_back)
    trade = after < before
    moved = trade & (head_at == count_of_heads - 1)
    initials = (queries, keys, values, output_gradient)
    incoming = passed_along(
        (queries[keep_rows:], keys[keep_rows:], values[keep_rows:], output_gradient[keep_rows:]),
        "seq",
        seq_count // 2,
    )
    query_rows, key_rows, value_rows, grad_rows = [
        jnp.concatenate([old[:keep_rows], jnp.where(moved, new, old[keep_rows:])], axis=0)
        for new, old in zip(incoming, initials)
    ]
    ids = jnp.where(trade & (place >= span - tail_rows), doc_ids(other_lengths, span), own_ids)
    heads = QUERY_HEAD_COUNT // count_of_heads
    group_count = KEY_VALUE_HEADS // count_of_heads
    qx, kx, vx, gx = (
        lax.all_to_all(query_rows, "head", split_axis=1, concat_axis=0, tiled=True),
        lax.all_to_all(key_rows, "head", split_axis=1, concat_axis=0, tiled=True),
        lax.all_to_all(value_rows, "head", split_axis=1, concat_axis=0, tiled=True),
        lax.all_to_all(grad_rows, "head", split_axis=1, concat_axis=0, tiled=True),
    )
    attention_output, query_gradient, key_gradient, value_gradient = attend(
        qx, kx, vx, gx, ids, place, ids, place, heads, group_count
    )
    results = (
        lax.all_to_all(attention_output, "head", split_axis=0, concat_axis=1, tiled=True),
        lax.all_to_all(query_gradient, "head", split_axis=0, concat_axis=1, tiled=True),
        lax.all_to_all(
            key_gradient.astype(jnp.bfloat16), "head", split_axis=0, concat_axis=1, tiled=True
        ),
        lax.all_to_all(
            value_gradient.astype(jnp.bfloat16), "head", split_axis=0, concat_axis=1, tiled=True
        ),
    )
    returned = passed_along(
        (
            results[0][keep_rows:],
            results[1][keep_rows:],
            results[2][keep_rows:],
            results[3][keep_rows:],
        ),
        "seq",
        seq_count // 2,
    )
    results = [
        jnp.concatenate([old[:keep_rows], jnp.where(moved, new, old[keep_rows:])], axis=0)
        for new, old in zip(returned, results)
    ]
    return (results[0], results[1], results[2], results[3])


def solution(mesh):
    in_specs = (
        P(("seq", "head"), None),
        P(("seq", "head"), None),
        P(("seq", "head"), None),
        P(("seq", "head"), None),
        P(),
    )
    out_specs = (
        P(("seq", "head"), None),
        P(("seq", "head"), None),
        P(("seq", "head"), None),
        P(("seq", "head"), None),
    )
    return jax.shard_map(body, mesh=mesh, in_specs=in_specs, out_specs=out_specs, check_vma=False)
```

profile of v0, /device:TPU:0, one launch (start us, length us, event | category | flops | bytes accessed | tf_op | source)
XLA Modules:
  0.0 497.1 jit_solution(8847307358862547012)
XLA Ops:
  1.9 4.0 collective-permute-start.1
  11.3 3.5 collective-permute-start
  14.8 2.9 fusion.41
  17.7 2.5 copy.134
  33.4 3.7 all-to-all-start.1
  38.3 8.5 %collective-permute-done = bf16[128,5120]{0,1:T(8,128)(2,1)} collective-permute-done((bf16[128,5120]{0,1:T(8,128)(2,1)}, bf16[128,5120]{0,1:T(8,128)(2,1)}, u32[]{:S(2)}, u32[]{:S(2)}) %collective-permute-start) | collective-permute-done | bytes 1310752 | tf_op jit(solution)/shard_map/ppermute | solution.py:19
  48.3 4.2 all-to-all-start.2
  54.4 5.2 %all-to-all-done.2 = bf16[256,2,512]{2,0,1:T(8,128)(2,1)} async-done(((bf16[256,2,512]{2,0,1:T(8,128)(2,1)}), bf16[256,2,512]{2,0,1:T(8,128)(2,1)}, u32[]{:S(2)}, u32[]{:S(2)}) %all-to-all-start.2) | async-done | bytes 524320 | tf_op jit(solution)/shard_map/all_to_all | solution.py:135
  59.5 3.9 all-to-all-start
  63.4 10.7 %collective-permute-done.3 = bf16[128,5120]{0,1:T(8,128)(2,1)} collective-permute-done((bf16[128,5120]{0,1:T(8,128)(2,1)}, bf16[128,5120]{0,1:T(8,128)(2,1)}, u32[]{:S(2)}, u32[]{:S(2)}) %collective-permute-start.3) | collective-permute-done | bytes 1310752 | tf_op jit(solution)/shard_map/ppermute | solution.py:19
  77.3 14.4 %all-to-all-done = bf16[256,2,2560]{0,2,1:T(8,128)(2,1)S(1)} async-done(((bf16[256,2,2560]{0,2,1:T(8,128)(2,1)}), bf16[256,2,2560]{0,2,1:T(8,128)(2,1)S(1)}, u32[]{:S(2)}, u32[]{:S(2)}) %all-to-all-start) | async-done | bytes 2621472 | tf_op jit(solution)/shard_map/all_to_all | solution.py:133
  91.8 5.2 %all-to-all-start.3 = ((bf16[256,2,2560]{0,2,1:T(8,128)(2,1)}), bf16[256,2,2560]{0,2,1:T(8,128)(2,1)}, u32[]{:S(2)}, u32[]{:S(2)}) async-start(bf16[256,2,2560]{0,2,1:T(8,128)(2,1)} %bitcast.130), calls=%async_computation.3 | async-start | bytes 5242880 | tf_op jit(solution)/shard_map/all_to_all | solution.py:136
  99.1 2.0 reshape.126
  103.0 17.2 %copy.96 = bf16[2,256,2560]{1,0,2:T(2,128)(2,1)} copy(bf16[2,256,2560]{1,2,0:T(8,128)(2,1)S(1)} %bitcast.128) | data formatting | bytes 5242880 | tf_op jit(solution)/shard_map/all_to_all | solution.py:133
  120.3 5.4 %reshape.124 = bf16[512,20,128]{0,2,1:T(8,128)(2,1)} reshape(bf16[2,256,2560]{1,0,2:T(2,128)(2,1)} %copy.96) | data formatting | bytes 5242880 | tf_op jit(solution)/shard_map/reshape | solution.py:69
  125.6 5.6 %copy.105 = bf16[2,256,2560]{1,0,2:T(2,128)(2,1)S(1)} copy(bf16[2,256,2560]{1,2,0:T(8,128)(2,1)} %bitcast.10) | data formatting | bytes 5242880 | tf_op jit(solution)/shard_map/all_to_all | solution.py:136
  131.2 3.4 reshape.127
  134.7 242.7 %while.17 = (s32[]{:T(128)}, bf16[20,512,128]{1,2,0:T(8,128)(2,1)}, bf16[20,512,128]{2,1,0:T(8,128)(2,1)}, f32[20,512,128]{2,1,0:T(8,128)}, f32[20,512,128]{2,1,...) while((s32[]{:T(128)}, bf16[20,512,128]{1,2,0:T(8,128)(2,1)}, ...), condition=%wide.region_12.13_spmd.clone, body=%wide.region_8.12_spmd.clone.sunk | while | flops 410516480 | bytes 11182331 | solution.py:80
  142.9 2.0 fusion.74
  144.9 1.9 fusion.73
  155.1 2.0 fusion.74
  167.2 2.0 fusion.74
  179.3 2.0 fusion.74
  191.4 2.0 fusion.74
  203.6 2.0 fusion.74
  205.5 1.9 fusion.73
  215.7 2.0 fusion.74
  227.8 2.0 fusion.74
  229.8 1.9 fusion.73
  240.0 1.9 fusion.74
  252.1 2.0 fusion.74
  264.2 2.0 fusion.74
  276.3 2.0 fusion.74
  288.5 2.0 fusion.74
  300.7 2.0 fusion.74
  312.8 2.0 fusion.74
  314.8 1.9 fusion.73
  324.9 2.0 fusion.74
  337.1 2.0 fusion.74
  349.2 2.0 fusion.74
  351.2 1.9 fusion.73
  361.3 2.0 fusion.74
  363.3 1.9 fusion.73
  373.5 2.0 fusion.74
  377.4 2.9 reduce_sum.97
  381.6 3.5 all-to-all-start.7
  385.1 2.9 reduce_sum.96
  389.4 2.3 all-to-all-done.7
  391.7 4.2 all-to-all-start.6
  395.9 3.5 all_to_all.104
  402.6 3.9 all-to-all-start.4
  406.4 4.4 copy.111
  410.8 4.9 all_to_all.107
  415.7 3.6 copy.112
  425.1 2.7 collective-permute-start.7
  428.7 3.0 all-to-all-done.4
  431.6 5.0 %all-to-all-start.5 = ((bf16[2,256,2560]{1,2,0:T(8,128)(2,1)}), bf16[2,256,2560]{1,2,0:T(8,128)(2,1)}, u32[]{:S(2)}, u32[]{:S(2)}) async-start(bf16[2,256,2560]{1,2,0:T(8,128)(2,1)} %copy.112), calls=%async_computation.5 | async-start | bytes 5242880 | tf_op jit(solution)/shard_map/all_to_all | solution.py:143
  436.6 1.9 fusion.40
  438.6 2.2 collective-permute-start.4
  443.0 18.0 %all-to-all-done.5 = bf16[2,256,2560]{1,2,0:T(8,128)(2,1)} async-done(((bf16[2,256,2560]{1,2,0:T(8,128)(2,1)}), bf16[2,256,2560]{1,2,0:T(8,128)(2,1)}, u32[]{:S(2)}, u32[]{:S(2)}) %all-to-all-start.5) | async-done | bytes 2621472 | tf_op jit(solution)/shard_map/all_to_all | solution.py:143
  461.0 3.4 fusion.39
  469.3 2.8 copy.119
  472.1 20.5 %collective-permute-done.5 = bf16[128,5120]{0,1:T(8,128)(2,1)} collective-permute-done((bf16[128,5120]{0,1:T(8,128)(2,1)}, bf16[128,5120]{0,1:T(8,128)(2,1)}, u32[]{:S(2)}, u32[]{:S(2)}) %collective-permute-start.5) | collective-permute-done | bytes 1310752 | tf_op jit(solution)/shard_map/ppermute | solution.py:19
  494.3 2.8 copy.120
  (301 shorter events, 200.2 us)
Async XLA Ops:
  1.9 30.5 %collective-permute-start.1 = (bf16[128,1024]{0,1:T(8,128)(2,1)S(1)}, bf16[128,1024]{0,1:T(8,128)(2,1)}, u32[]{:S(2)}, u32[]{:S(2)}) collective-permute-start(bf16[128,1024]{0,1:T(8,128)(2,1)S(1)} %copy.130), channel_id=1, source_target_pairs={{64,0},{66,2},{68,4},{70,6},{72,8},{74,10},{76,12},{78,14},{80,16}... | collective-permute-start | bytes 786440 | tf_op jit(solution)/shard_map/ppermute | solution.py:19
  7.9 29.3 %collective-permute-start.2 = (bf16[128,1024]{0,1:T(8,128)(2,1)S(1)}, bf16[128,1024]{0,1:T(8,128)(2,1)}, u32[]{:S(2)}, u32[]{:S(2)}) collective-permute-start(bf16[128,1024]{0,1:T(8,128)(2,1)S(1)} %copy.132), channel_id=1, source_target_pairs={{64,0},{66,2},{68,4},{70,6},{72,8},{74,10},{76,12},{78,14},{80,16}... | collective-permute-start | bytes 786440 | tf_op jit(solution)/shard_map/ppermute | solution.py:19
  11.3 35.6 %collective-permute-start = (bf16[128,5120]{0,1:T(8,128)(2,1)}, bf16[128,5120]{0,1:T(8,128)(2,1)}, u32[]{:S(2)}, u32[]{:S(2)}) collective-permute-start(bf16[128,5120]{0,1:T(8,128)(2,1)} %copy.128), channel_id=1, source_target_pairs={{64,0},{66,2},{68,4},{70,6},{72,8},{74,10},{76,12},{78,14},{80,16}... | collective-permute-start | bytes 3932168 | tf_op jit(solution)/shard_map/ppermute | solution.py:19
  17.7 2.5 copy-start.8
  20.2 53.9 %collective-permute-start.3 = (bf16[128,5120]{0,1:T(8,128)(2,1)}, bf16[128,5120]{0,1:T(8,128)(2,1)}, u32[]{:S(2)}, u32[]{:S(2)}) collective-permute-start(bf16[128,5120]{0,1:T(8,128)(2,1)} %copy.134), channel_id=1, source_target_pairs={{64,0},{66,2},{68,4},{70,6},{72,8},{74,10},{76,12},{78,14},{80,16}... | collective-permute-start | bytes 3932168 | tf_op jit(solution)/shard_map/ppermute | solution.py:19
  29.5 2.9 copy-start.6
  32.3 4.9 copy-start.4
  33.4 14.9 %all-to-all-start.1 = ((bf16[256,2,512]{2,0,1:T(8,128)(2,1)}), bf16[256,2,512]{2,0,1:T(8,128)(2,1)S(1)}, u32[]{:S(2)}, u32[]{:S(2)}) async-start(bf16[256,2,512]{2,0,1:T(8,128)(2,1)} %copy.99), calls=%async_computation.1 | async-start | bytes 1048576 | tf_op jit(solution)/shard_map/all_to_all | solution.py:134
  38.3 14.3 %copy-start.3 = (bf16[128,5120]{0,1:T(8,128)(2,1)S(1)}, bf16[128,5120]{0,1:T(8,128)(2,1)}, u32[]{:S(2)}) copy-start(bf16[128,5120]{0,1:T(8,128)(2,1)} %copy.125) | copy-start | bytes 3932164
  48.3 11.2 %all-to-all-start.2 = ((bf16[256,2,512]{2,0,1:T(8,128)(2,1)}), bf16[256,2,512]{2,0,1:T(8,128)(2,1)}, u32[]{:S(2)}, u32[]{:S(2)}) async-start(bf16[256,2,512]{2,0,1:T(8,128)(2,1)} %copy.102), calls=%async_computation.2 | async-start | bytes 1048576 | tf_op jit(solution)/shard_map/all_to_all | solution.py:135
  59.5 32.3 %all-to-all-start = ((bf16[256,2,2560]{0,2,1:T(8,128)(2,1)}), bf16[256,2,2560]{0,2,1:T(8,128)(2,1)S(1)}, u32[]{:S(2)}, u32[]{:S(2)}) async-start(bf16[256,2,2560]{0,2,1:T(8,128)(2,1)} %bitcast.131), calls=%async_computation | async-start | bytes 5242880 | tf_op jit(solution)/shard_map/all_to_all | solution.py:133
  63.4 12.2 %copy-start.2 = (bf16[128,5120]{0,1:T(8,128)(2,1)S(1)}, bf16[128,5120]{0,1:T(8,128)(2,1)}, u32[]{:S(2)}) copy-start(bf16[128,5120]{0,1:T(8,128)(2,1)} %copy.133) | copy-start | bytes 3932164
  91.8 33.8 %all-to-all-start.3 = ((bf16[256,2,2560]{0,2,1:T(8,128)(2,1)}), bf16[256,2,2560]{0,2,1:T(8,128)(2,1)}, u32[]{:S(2)}, u32[]{:S(2)}) async-start(bf16[256,2,2560]{0,2,1:T(8,128)(2,1)} %bitcast.130), calls=%async_computation.3 | async-start | bytes 5242880 | tf_op jit(solution)/shard_map/all_to_all | solution.py:136
  134.7 4.0 copy-start.7
  146.8 4.0 copy-start.7
  159.0 4.0 copy-start.7
  171.1 4.0 copy-start.7
  183.2 4.0 copy-start.7
  195.3 4.0 copy-start.7
  207.5 4.0 copy-start.7
  219.6 4.0 copy-start.7
  231.7 4.0 copy-start.7
  243.8 4.0 copy-start.7
  255.9 4.0 copy-start.7
  268.1 4.0 copy-start.7
  280.2 4.0 copy-start.7
  292.4 4.0 copy-start.7
  304.5 4.0 copy-start.7
  316.7 4.0 copy-start.7
  328.8 4.0 copy-start.7
  340.9 4.0 copy-start.7
  353.1 4.0 copy-start.7
  365.2 4.0 copy-start.7
  381.6 10.1 %all-to-all-start.7 = ((bf16[2,256,512]{2,1,0:T(8,128)(2,1)}), bf16[2,256,512]{2,1,0:T(8,128)(2,1)S(1)}, u32[]{:S(2)}, u32[]{:S(2)}) async-start(bf16[2,256,512]{2,1,0:T(8,128)(2,1)} %convert_element_type.51), calls=%async_computation.7 | async-start | bytes 1048576 | tf_op jit(solution)/shard_map/all_to_all | solution.py:147
  391.7 10.9 %all-to-all-start.6 = ((bf16[2,256,512]{2,1,0:T(8,128)(2,1)}), bf16[2,256,512]{2,1,0:T(8,128)(2,1)}, u32[]{:S(2)}, u32[]{:S(2)}) async-start(bf16[2,256,512]{2,1,0:T(8,128)(2,1)} %convert_element_type.48), calls=%async_computation.6 | async-start | bytes 1048576 | tf_op jit(solution)/shard_map/all_to_all | solution.py:144
  402.6 29.1 %all-to-all-start.4 = ((bf16[2,256,2560]{1,2,0:T(8,128)(2,1)}), bf16[2,256,2560]{1,2,0:T(8,128)(2,1)S(1)}, u32[]{:S(2)}, u32[]{:S(2)}) async-start(bf16[2,256,2560]{1,2,0:T(8,128)(2,1)} %copy.110), calls=%async_computation.4 | async-start | bytes 5242880 | tf_op jit(solution)/shard_map/all_to_all | solution.py:142
  425.1 15.6 %collective-permute-start.7 = (bf16[128,1024]{0,1:T(8,128)(2,1)}, bf16[128,1024]{0,1:T(8,128)(2,1)}, u32[]{:S(2)}, u32[]{:S(2)}) collective-permute-start(bf16[128,1024]{0,1:T(8,128)(2,1)} %bitcast.151), channel_id=1, source_target_pairs={{64,0},{66,2},{68,4},{70,6},{72,8},{74,10},{76,12},{78,14},{80,16}... | collective-permute-start | bytes 786440 | tf_op jit(solution)/shard_map/ppermute | solution.py:19
  427.8 14.0 %collective-permute-start.6 = (bf16[128,1024]{0,1:T(8,128)(2,1)S(1)}, bf16[128,1024]{0,1:T(8,128)(2,1)}, u32[]{:S(2)}, u32[]{:S(2)}) collective-permute-start(bf16[128,1024]{0,1:T(8,128)(2,1)S(1)} %bitcast.150), channel_id=1, source_target_pairs={{64,0},{66,2},{68,4},{70,6},{72,8},{74,10},{76,12},{78,14},{80,16}... | collective-permute-start | bytes 786440 | tf_op jit(solution)/shard_map/ppermute | solution.py:19
  431.6 29.4 %all-to-all-start.5 = ((bf16[2,256,2560]{1,2,0:T(8,128)(2,1)}), bf16[2,256,2560]{1,2,0:T(8,128)(2,1)}, u32[]{:S(2)}, u32[]{:S(2)}) async-start(bf16[2,256,2560]{1,2,0:T(8,128)(2,1)} %copy.112), calls=%async_computation.5 | async-start | bytes 5242880 | tf_op jit(solution)/shard_map/all_to_all | solution.py:143
  436.6 4.1 copy-start.5
  438.6 28.9 %collective-permute-start.4 = (bf16[128,5120]{0,1:T(8,128)(2,1)}, bf16[128,5120]{0,1:T(8,128)(2,1)S(1)}, u32[]{:S(2)}, u32[]{:S(2)}) collective-permute-start(bf16[128,5120]{0,1:T(8,128)(2,1)} %bitcast.17), channel_id=1, source_target_pairs={{64,0},{66,2},{68,4},{70,6},{72,8},{74,10},{76,12},{78,14},{80,16}... | collective-permute-start | bytes 3932168 | tf_op jit(solution)/shard_map/ppermute | solution.py:19
  464.4 4.6 copy-start
  464.4 28.2 %collective-permute-start.5 = (bf16[128,5120]{0,1:T(8,128)(2,1)}, bf16[128,5120]{0,1:T(8,128)(2,1)}, u32[]{:S(2)}, u32[]{:S(2)}) collective-permute-start(bf16[128,5120]{0,1:T(8,128)(2,1)} %bitcast.21), channel_id=1, source_target_pairs={{64,0},{66,2},{68,4},{70,6},{72,8},{74,10},{76,12},{78,14},{80,16}... | collective-permute-start | bytes 3932168 | tf_op jit(solution)/shard_map/ppermute | solution.py:19
  472.1 22.0 %copy-start.1 = (bf16[128,2,2560]{0,2,1:T(8,128)(2,1)S(1)}, bf16[128,2,2560]{0,2,1:T(8,128)(2,1)}, u32[]{:S(2)}) copy-start(bf16[128,2,2560]{0,2,1:T(8,128)(2,1)} %get-tuple-element.190) | copy-start | bytes 3932164
where the time goes:
time: 502 us; the launch traced here: 497 us
  matrix products  168 us (33%)
  local copies, waits for them, and re-layouts  109 us (22%)
  waiting for transfers between devices  85.4 us (17%)
  starting transfers between devices  48.5 us (10%)
  other arithmetic  40.9 us (8%)
  loops' own time  39.2 us (8%)
  between operations  6.18 us (1%)
    ppermute x8, waiting for transfers between devices, passed_along(): return lax.ppermute(block, axis, route)  41.3 us
    dot_general x20, matrix products, head_pass(): jnp.dot(probs_bf.T, grad_head, preferred_element_type=jnp.float32)  39.4 us
    another operation x1, loops' own time, attend(): lax.map(per_head, (query_heads, grad_heads, group_of))  39.2 us
    dot_general x20, matrix products, head_pass(): jnp.dot(dscores.T, query_head, preferred_element_type=jnp.float32) * scale  38.1 us
    dot_general x20, matrix products, head_pass(): jnp.dot(grad_head, value_head.T, preferred_element_type=jnp.float32)  25.5 us
    dot_general x20, matrix products, head_pass(): jnp.dot(query_head, key_head.T, preferred_element_type=jnp.float32) * scale  24.8 us
    unnamed x32, local copies, waits for them, and re-layouts  20.5 us
    dot_general x20, matrix products, head_pass(): jnp.dot(dscores, key_head, preferred_element_type=jnp.float32) * scale  20.2 us
  transfers between devices with their start and end apart: 16, of which 10 were waited for; matrix products, arithmetic and copies ran while one was open for 17% of the time, Pallas kernels for 0%

commit v1 on v0

v1 whole, which is shorter than its diff:
```python
import functools
import math

import jax
import jax.numpy as jnp
from jax import lax
from jax.experimental import pallas as pl
from jax.experimental.pallas import tpu as pltpu
from jax.sharding import PartitionSpec as P

QUERY_HEADS = 40
GROUPS = 8
RATIO = QUERY_HEADS // GROUPS
WIDTH = 128
WIDE = RATIO * WIDTH
ROWS = 256
HALF = 128
DOCS = 16
NEG = -1e30
SCALE = 1.0 / math.sqrt(WIDTH)
TO_EXP2 = SCALE * math.log2(math.e)
MESH = pl.DeviceIdType.MESH
F32 = jnp.float32
BF16 = jnp.bfloat16


def dot_nt(a, b):
    return lax.dot_general(a, b, (((1,), (1,)), ((), ())), preferred_element_type=F32)


def dot_nn(a, b):
    return jnp.dot(a, b, preferred_element_type=F32)


def stacked(ref, row, group):
    return jnp.concatenate(
        [
            ref[pl.ds(row, HALF), pl.ds(pl.multiple_of(group * WIDE + h * WIDTH, WIDTH), WIDTH)]
            for h in range(RATIO)
        ],
        axis=0,
    )


def columns(group):
    return pl.ds(pl.multiple_of(group * WIDTH, WIDTH), WIDTH)


def probabilities(keys, queries, bias):
    logits = dot_nt(keys, queries) * TO_EXP2 + jnp.concatenate([bias] * RATIO, axis=1)
    weights = jnp.exp2(logits - jnp.max(logits, axis=0, keepdims=True))
    return weights * (1.0 / jnp.sum(weights, axis=0, keepdims=True))


def score_gradient(probs, values, grads):
    dprobs = dot_nt(values, grads)
    delta = jnp.sum(probs * dprobs, axis=0, keepdims=True)
    return (probs * (dprobs - delta)).astype(BF16)


def put_heads(ref, row, group, transposed):
    for h in range(RATIO):
        block = transposed[:, h * WIDTH : (h + 1) * WIDTH].T
        where = pl.ds(pl.multiple_of(group * WIDE + h * WIDTH, WIDTH), WIDTH)
        ref[pl.ds(row, HALF), where] = block.astype(BF16)


def mask_bias(lengths, block, first_query, first_key, keys):
    query = first_query + lax.broadcasted_iota(jnp.int32, (1, HALF), 1)
    start = jnp.int32(0)
    doc_start = jnp.zeros((1, HALF), jnp.int32)
    for d in range(DOCS):
        doc_start = jnp.where(query >= start, start, doc_start)
        start = start + lengths[block, d]
    key = first_key + lax.broadcasted_iota(jnp.int32, (keys, HALF), 0)
    return jnp.where((key >= doc_start) & (key <= query), 0.0, NEG).astype(F32)


def kernel(
    lengths_hbm, q_hbm, k_hbm, v_hbm, g_hbm,
    o_out, dq_out, dk_out, dv_out,
    q_own, k_own, v_own, g_own,
    k_far, v_far, dk_send, dv_send, dk_far, dv_far, dk_sum, dv_sum,
    bias_a, bias_b, lengths, lengths_sem, load_sem, send_sem, recv_sem,
):
    seq = lax.axis_index("seq")
    head = lax.axis_index("head")
    partner = (seq, 1 - head)
    barrier = pltpu.get_barrier_semaphore()
    pl.semaphore_signal(barrier, inc=1, device_id=partner, device_id_type=MESH)

    lengths_copy = pltpu.make_async_copy(lengths_hbm, lengths, lengths_sem)
    lengths_copy.start()

    def loads(g):
        wide = pl.ds(pl.multiple_of(g * WIDE, WIDTH), WIDE)
        return [
            pltpu.make_async_copy(src.at[:, where], dst.at[:, where], load_sem.at[i, g])
            for i, (src, dst, where) in enumerate(
                (
                    (k_hbm, k_own, columns(g)),
                    (q_hbm, q_own, wide),
                    (g_hbm, g_own, wide),
                    (v_hbm, v_own, columns(g)),
                )
            )
        ]

    def far(i, g):
        src, dst = (
            (k_hbm.at[:, columns(g)], k_far.at[g]),
            (v_hbm.at[:, columns(g)], v_far.at[g]),
            (dv_send.at[g], dv_far.at[g]),
            (dk_send.at[g], dk_far.at[g]),
        )[i]
        return pltpu.make_async_remote_copy(
            src_ref=src,
            dst_ref=dst,
            send_sem=send_sem.at[i, g],
            recv_sem=recv_sem.at[i, g],
            device_id=partner,
            device_id_type=MESH,
        )

    def start_loads(g, _):
        for copy in loads(g):
            copy.start()
        return 0

    lax.fori_loop(0, GROUPS, start_loads, 0)
    lengths_copy.wait()
    pl.semaphore_wait(barrier, 1)

    @pl.when(head == 0)
    def _():
        def send(g, _):
            far(0, g).start()
            far(1, g).start()
            return 0

        lax.fori_loop(0, GROUPS, send, 0)
        bias_a[0:ROWS] = mask_bias(lengths, seq, HALF, 0, ROWS)
        bias_b[...] = mask_bias(lengths, seq, 0, 0, HALF)

        def local(g, _):
            for copy in loads(g):
                copy.wait()
            for row, keys, bias in ((HALF, ROWS, bias_a), (0, HALF, bias_b)):
                kk = k_own[0:keys, columns(g)]
                vv = v_own[0:keys, columns(g)]
                qq = stacked(q_own, row, g)
                gg = stacked(g_own, row, g)
                probs = probabilities(kk, qq, bias[0:keys])
                rounded = probs.astype(BF16)
                dscores = score_gradient(probs, vv, gg)
                dv = dot_nn(rounded, gg)
                dk = dot_nn(dscores, qq)
                if row:
                    dv_sum[g] = dv
                    dk_sum[g] = dk
                else:
                    dv_sum[g, 0:HALF] += dv
                    dk_sum[g, 0:HALF] += dk
                put_heads(o_out, row, g, dot_nn(vv.T, rounded))
                put_heads(dq_out, row, g, dot_nn(kk.T, dscores) * SCALE)
            return 0

        lax.fori_loop(0, GROUPS, local, 0)

        def finish(g, _):
            far(2, g).wait_recv()
            dv_out[:, columns(g)] = (dv_sum[g] + dv_far[g].astype(F32)).astype(BF16)
            far(3, g).wait_recv()
            dk_out[:, columns(g)] = (dk_sum[g] * SCALE + dk_far[g].astype(F32)).astype(BF16)
            return 0

        lax.fori_loop(0, GROUPS, finish, 0)

        def drain(g, _):
            far(0, g).wait_send()
            far(1, g).wait_send()
            return 0

        lax.fori_loop(0, GROUPS, drain, 0)

    @pl.when(head == 1)
    def _():
        bias_a[...] = mask_bias(lengths, seq, ROWS, 0, ROWS + HALF)
        bias_b[...] = mask_bias(lengths, seq, ROWS + HALF, ROWS + HALF, HALF)

        def work(g, _):
            for copy in loads(g):
                copy.wait()
            kk = k_own[HALF:ROWS, columns(g)]
            vv = v_own[HALF:ROWS, columns(g)]
            qq = stacked(q_own, HALF, g)
            gg = stacked(g_own, HALF, g)
            probs = probabilities(kk, qq, bias_b[...])
            rounded = probs.astype(BF16)
            dscores = score_gradient(probs, vv, gg)
            dv_out[HALF:ROWS, columns(g)] = dot_nn(rounded, gg).astype(BF16)
            dk_out[HALF:ROWS, columns(g)] = (dot_nn(dscores, qq) * SCALE).astype(BF16)
            put_heads(o_out, HALF, g, dot_nn(vv.T, rounded))
            put_heads(dq_out, HALF, g, dot_nn(kk.T, dscores) * SCALE)

            far(0, g).wait_recv()
            kk = jnp.concatenate([k_far[g], k_own[0:HALF, columns(g)]], axis=0)
            qq = stacked(q_own, 0, g)
            gg = stacked(g_own, 0, g)
            probs = probabilities(kk, qq, bias_a[...])
            rounded = probs.astype(BF16)
            dv = dot_nn(rounded, gg).astype(BF16)
            dv_send[g] = dv[0:ROWS]
            far(2, g).start()
            dv_out[0:HALF, columns(g)] = dv[ROWS:]
            far(1, g).wait_recv()
            vv = jnp.concatenate([v_far[g], v_own[0:HALF, columns(g)]], axis=0)
            dscores = score_gradient(probs, vv, gg)
            dk = (dot_nn(dscores, qq) * SCALE).astype(BF16)
            dk_send[g] = dk[0:ROWS]
            far(3, g).start()
            dk_out[0:HALF, columns(g)] = dk[ROWS:]
            put_heads(o_out, 0, g, dot_nn(vv.T, rounded))
            put_heads(dq_out, 0, g, dot_nn(kk.T, dscores) * SCALE)
            return 0

        lax.fori_loop(0, GROUPS, work, 0)

        def drain(g, _):
            far(2, g).wait_send()
            far(3, g).wait_send()
            return 0

        lax.fori_loop(0, GROUPS, drain, 0)


def body(queries, keys, values, output_gradient, document_lengths):
    hbm = pl.BlockSpec(memory_space=pl.ANY)
    block = pltpu.VMEM((GROUPS, ROWS, WIDTH), BF16)
    total = pltpu.VMEM((GROUPS, ROWS, WIDTH), F32)
    return pl.pallas_call(
        kernel,
        out_shape=[pltpu.VMEM(x.shape, BF16) for x in (queries, queries, keys, values)],
        in_specs=[hbm] * 5,
        scratch_shapes=[
            pltpu.VMEM(queries.shape, BF16),
            pltpu.VMEM(keys.shape, BF16),
            pltpu.VMEM(values.shape, BF16),
            pltpu.VMEM(queries.shape, BF16),
            block, block, block, block, block, block, total, total,
            pltpu.VMEM((ROWS + HALF, HALF), F32),
            pltpu.VMEM((HALF, HALF), F32),
            pltpu.SMEM(document_lengths.shape, jnp.int32),
            pltpu.SemaphoreType.DMA,
            pltpu.SemaphoreType.DMA((4, GROUPS)),
            pltpu.SemaphoreType.DMA((4, GROUPS)),
            pltpu.SemaphoreType.DMA((4, GROUPS)),
        ],
        compiler_params=pltpu.CompilerParams(
            collective_id=0, has_side_effects=True, vmem_limit_bytes=54 << 20
        ),
        name="packed_attention",
    )(document_lengths, queries, keys, values, output_gradient)


def solution(mesh):
    rows = P(("seq", "head"), None)
    return jax.shard_map(
        body,
        mesh=mesh,
        in_specs=(rows, rows, rows, rows, P()),
        out_specs=(rows, rows, rows, rows),
        check_vma=False,
    )
```

time: 502 us -> 37.9 us (0.08)
  matrix products: 168 us -> 0 us
  local copies, waits for them, and re-layouts: 109 us -> 5.97 us
  waiting for transfers between devices: 85.4 us -> 0 us
  starting transfers between devices: 48.5 us -> 0 us
  other arithmetic: 40.9 us -> 0 us
  loops' own time: 39.2 us -> 0 us
  Pallas kernels: 0 us -> 31.2 us
  between operations: 6.18 us -> 0.64 us
    dot_general x120 -> x0, matrix products: 168 us -> none  [the longest x20 39.4 us: head_pass(): jnp.dot(probs_bf.T, grad_head, preferred_element_type=jnp.float32)]
    all_to_all x8 -> x0, waiting for transfers between devices: 44.1 us -> none  [the longest x1 18 us: body(): lax.all_to_all(query_gradient, 'head', split_axis=0, concat_axis=1, tiled...]
    ppermute x8 -> x0, waiting for transfers between devices: 41.3 us -> none  [passed_along(): return lax.ppermute(block, axis, route)]
    another operation x1 -> x0, loops' own time: 39.2 us -> none  [attend(): lax.map(per_head, (query_heads, grad_heads, group_of))]
    all_to_all x8 -> x0, local copies, waits for them, and re-layouts: 38.7 us -> none  [the longest x1 17.2 us: body(): lax.all_to_all(query_rows, 'head', split_axis=1, concat_axis=0, tiled=True)]
    all_to_all x8 -> x0, starting transfers between devices: 33.6 us -> none  [the longest x1 5.17 us: body(): lax.all_to_all(grad_rows, 'head', split_axis=1, concat_axis=0, tiled=True)]
    pallas_call x0 -> x1, Pallas kernels: none -> 31.2 us  [body(): pl.pallas_call(kernel, out_shape=[pltpu.VMEM(x.shape, BF16) for x in (que...]
    reduce_sum x44 -> x0, other arithmetic: 29.9 us -> none  [the longest x20 19.4 us: head_pass(): jnp.sum(grad_head.astype(jnp.float32) * attention_output.astype(jnp.float...]
  transfers between devices with their start and end apart: 16 -> 0, of which waited for: 10 -> 0; matrix products, arithmetic and copies ran while one was open for 17% -> 0% of each run, Pallas kernels for 0% -> 0%
where the time goes in v1:
time: 37.9 us; the launch traced here: 37.8 us
  Pallas kernels  31.2 us (82%)
  local copies, waits for them, and re-layouts  5.97 us (16%)
  between operations  0.64 us (2%)
    pallas_call x1, Pallas kernels, body(): pl.pallas_call(kernel, out_shape=[pltpu.VMEM(x.shape, BF16) for x in (que...  31.2 us
    unnamed x5, local copies, waits for them, and re-layouts  5.97 us

profile of v1, /device:TPU:0, one launch (start us, length us, event | category | flops | bytes accessed | tf_op | source)
XLA Modules:
  0.0 37.8 jit_solution(6531788372189587642)
XLA Ops:
  0.6 1.4 %copy.9.lengths_hbm = s32[64,16]{1,0:T(8,128)} copy(s32[64,16]{0,1:T(8,128)} %param.9) | data formatting | bytes 8192 | tf_op args[4]
  2.0 31.2 %packed_attention.1 = (bf16[256,5120]{1,0:T(8,128)(2,1)S(1)}, bf16[256,5120]{1,0:T(8,128)(2,1)S(1)}, bf16[256,1024]{1,0:T(8,128)(2,1)S(1)}, bf16[256,1024]{1,0:T(8,128)(2,1)S(1)}) custom-call(s32[64,16]{1,0:T(8,128)} %copy.9.lengths_hbm, bf16[256,5120]{1,0:T(8,128)(2,1)} %q_hbm.1, bf16[256,1024]{1,0:T(8,128)(2,1)} %k_hbm.1, bf16[256,1024]{1,0:T(8,128)(2,1)} %v_hbm.1, ...), custom_call_target="tpu_custom_call" | custom-call | tf_op jit(solution)/shard_map/packed_attention/pallas_call | solution.py:241
  33.2 1.5 %copy.14 = bf16[256,5120]{1,0:T(8,128)(2,1)} copy(bf16[256,5120]{1,0:T(8,128)(2,1)S(1)} %get-tuple-element.4) | data formatting | bytes 5242880
  34.7 0.8 %copy.16 = bf16[256,1024]{1,0:T(8,128)(2,1)} copy(bf16[256,1024]{1,0:T(8,128)(2,1)S(1)} %get-tuple-element.6) | data formatting | bytes 1048576
  35.5 0.8 %copy.17 = bf16[256,1024]{1,0:T(8,128)(2,1)} copy(bf16[256,1024]{1,0:T(8,128)(2,1)S(1)} %get-tuple-element.7) | data formatting | bytes 1048576
  36.3 1.5 %copy.15 = bf16[256,5120]{1,0:T(8,128)(2,1)} copy(bf16[256,5120]{1,0:T(8,128)(2,1)S(1)} %get-tuple-element.5) | data formatting | bytes 5242880

commit v2 on v1

--- a/solution.py
+++ b/solution.py
@@ -71,7 +71,7 @@
     doc_start = jnp.zeros((1, HALF), jnp.int32)
     for d in range(DOCS):
         doc_start = jnp.where(query >= start, start, doc_start)
-        start = start + lengths[block, d]
+        start = start + lengths[d, block]
     key = first_key + lax.broadcasted_iota(jnp.int32, (keys, HALF), 0)
     return jnp.where((key >= doc_start) & (key <= query), 0.0, NEG).astype(F32)
 
@@ -234,11 +234,22 @@
         lax.fori_loop(0, GROUPS, drain, 0)
 
 
+def store_kernel(*refs):
+    count = len(refs) // 2
+    copies = [
+        pltpu.make_async_copy(refs[i], refs[count + i], refs[-1].at[i]) for i in range(count)
+    ]
+    for copy in copies:
+        copy.start()
+    for copy in copies:
+        copy.wait()
+
+
 def body(queries, keys, values, output_gradient, document_lengths):
     hbm = pl.BlockSpec(memory_space=pl.ANY)
     block = pltpu.VMEM((GROUPS, ROWS, WIDTH), BF16)
     total = pltpu.VMEM((GROUPS, ROWS, WIDTH), F32)
-    return pl.pallas_call(
+    results = pl.pallas_call(
         kernel,
         out_shape=[pltpu.VMEM(x.shape, BF16) for x in (queries, queries, keys, values)],
         in_specs=[hbm] * 5,
@@ -250,7 +261,7 @@
             block, block, block, block, block, block, total, total,
             pltpu.VMEM((ROWS + HALF, HALF), F32),
             pltpu.VMEM((HALF, HALF), F32),
-            pltpu.SMEM(document_lengths.shape, jnp.int32),
+            pltpu.SMEM(document_lengths.shape[::-1], jnp.int32),
             pltpu.SemaphoreType.DMA,
             pltpu.SemaphoreType.DMA((4, GROUPS)),
             pltpu.SemaphoreType.DMA((4, GROUPS)),
@@ -260,7 +271,16 @@
             collective_id=0, has_side_effects=True, vmem_limit_bytes=54 << 20
         ),
         name="packed_attention",
-    )(document_lengths, queries, keys, values, output_gradient)
+    )(document_lengths.T, queries, keys, values, output_gradient)
+    return pl.pallas_call(
+        store_kernel,
+        out_shape=[jax.ShapeDtypeStruct(x.shape, BF16) for x in results],
+        in_specs=[pl.BlockSpec(memory_space=pltpu.VMEM)] * len(results),
+        out_specs=[hbm] * len(results),
+        scratch_shapes=[pltpu.SemaphoreType.DMA((len(results),))],
+        compiler_params=pltpu.CompilerParams(vmem_limit_bytes=16 << 20),
+        name="store_results",
+    )(*[pltpu.with_memory_space_constraint(x, pltpu.VMEM) for x in results])
 
 
 def solution(mesh):

time: 37.9 us -> 34.8 us (0.918)
  local copies, waits for them, and re-layouts: 5.97 us -> 0 us
  Pallas kernels: 31.2 us -> 34 us
    unnamed x5 -> x0, local copies, waits for them, and re-layouts: 5.97 us -> none
    pallas_call x0 -> x1, Pallas kernels: none -> 2.71 us  [body(): pl.pallas_call(store_kernel, out_shape=[jax.ShapeDtypeStruct(x.shape, BF1...]
where the time goes in v2:
time: 34.8 us; the launch traced here: 34.6 us
  Pallas kernels  34 us (98%)
  between operations  0.64 us (2%)
    pallas_call x1, Pallas kernels, body(): pl.pallas_call(kernel, out_shape=[pltpu.VMEM(x.shape, BF16) for x in (que...  31.3 us
    pallas_call x1, Pallas kernels, body(): pl.pallas_call(store_kernel, out_shape=[jax.ShapeDtypeStruct(x.shape, BF1...  2.71 us

profile of v2, /device:TPU:0, one launch (start us, length us, event | category | flops | bytes accessed | tf_op | source)
XLA Modules:
  0.0 34.6 jit_solution(3861248785386723831)
XLA Ops:
  0.6 31.3 %packed_attention.1 = (bf16[256,5120]{1,0:T(8,128)(2,1)S(1)}, bf16[256,5120]{1,0:T(8,128)(2,1)S(1)}, bf16[256,1024]{1,0:T(8,128)(2,1)S(1)}, bf16[256,1024]{1,0:T(8,128)(2,1)S(1)}) custom-call(s32[16,64]{1,0:T(8,128)} %bitcast.1, bf16[256,5120]{1,0:T(8,128)(2,1)} %q_hbm.1, bf16[256,1024]{1,0:T(8,128)(2,1)} %k_hbm.1, bf16[256,1024]{1,0:T(8,128)(2,1)} %v_hbm.1, ...), custom_call_target="tpu_custom_call" | custom-call | tf_op jit(solution)/shard_map/packed_attention/pallas_call | solution.py:252
  31.9 2.7 %store_results.1 = (bf16[256,5120]{1,0:T(8,128)(2,1)}, bf16[256,5120]{1,0:T(8,128)(2,1)}, bf16[256,1024]{1,0:T(8,128)(2,1)}, bf16[256,1024]{1,0:T(8,128)(2,1)}) custom-call(bf16[256,5120]{1,0:T(8,128)(2,1)S(1)} %get-tuple-element.8.refs_0_, bf16[256,5120]{1,0:T(8,128)(2,1)S(1)} %get-tuple-element.9.refs_1_, bf16[256,1024]{1,0:T(8,128)(2,1)S(1)} %get-tuple-element.10.refs_2_, ...), custom_call_target="tpu_custom_call" | custom-call | tf_op jit(solution)/shard_map/store_results/pallas_call | solution.py:275

commit v3 on v2

--- a/solution.py
+++ b/solution.py
@@ -19,6 +19,7 @@
 NEG = -1e30
 SCALE = 1.0 / math.sqrt(WIDTH)
 TO_EXP2 = SCALE * math.log2(math.e)
+LEAD = 1
 MESH = pl.DeviceIdType.MESH
 F32 = jnp.float32
 BF16 = jnp.bfloat16
@@ -44,6 +45,18 @@
 
 def columns(group):
     return pl.ds(pl.multiple_of(group * WIDTH, WIDTH), WIDTH)
+
+
+PARTS = [slice(0, 256), slice(256, 512), slice(512, 640)]
+
+
+def wide(parts):
+    return jnp.concatenate([x.astype(BF16) for x in parts], axis=1)
+
+
+def logits(keys, queries, bias):
+    heads = queries.shape[0] // WIDTH
+    return dot_nt(keys, queries) * TO_EXP2 + jnp.concatenate([bias] * heads, axis=1)
 
 
 def probabilities(keys, queries, bias):
@@ -85,31 +98,22 @@
 ):
     seq = lax.axis_index("seq")
     head = lax.axis_index("head")
+    core = lax.rem(seq, 2)
     partner = (seq, 1 - head)
     barrier = pltpu.get_barrier_semaphore()
     pl.semaphore_signal(barrier, inc=1, device_id=partner, device_id_type=MESH)
 
     lengths_copy = pltpu.make_async_copy(lengths_hbm, lengths, lengths_sem)
-    lengths_copy.start()
-
-    def loads(g):
-        wide = pl.ds(pl.multiple_of(g * WIDE, WIDTH), WIDE)
-        return [
-            pltpu.make_async_copy(src.at[:, where], dst.at[:, where], load_sem.at[i, g])
-            for i, (src, dst, where) in enumerate(
-                (
-                    (k_hbm, k_own, columns(g)),
-                    (q_hbm, q_own, wide),
-                    (g_hbm, g_own, wide),
-                    (v_hbm, v_own, columns(g)),
-                )
-            )
-        ]
+
+    def load(i, g):
+        src, dst = ((k_hbm, k_own), (v_hbm, v_own), (q_hbm, q_own), (g_hbm, g_own))[i]
+        where = columns(g) if i < 2 else pl.ds(pl.multiple_of(g * WIDE, WIDTH), WIDE)
+        return pltpu.make_async_copy(src.at[:, where], dst.at[:, where], load_sem.at[i, g])
 
     def far(i, g):
         src, dst = (
-            (k_hbm.at[:, columns(g)], k_far.at[g]),
-            (v_hbm.at[:, columns(g)], v_far.at[g]),
+            (k_own.at[:, columns(g)], k_far.at[g]),
+            (v_own.at[:, columns(g)], v_far.at[g]),
             (dv_send.at[g], dv_far.at[g]),
             (dk_send.at[g], dk_far.at[g]),
         )[i]
@@ -122,29 +126,49 @@
             device_id_type=MESH,
         )
 
-    def start_loads(g, _):
-        for copy in loads(g):
-            copy.start()
+    def start_key_loads(g, _):
+        load(0, g).start()
+        load(1, g).start()
         return 0
 
-    lax.fori_loop(0, GROUPS, start_loads, 0)
-    lengths_copy.wait()
-    pl.semaphore_wait(barrier, 1)
+    def start_query_loads(g, _):
+        load(2, g).start()
+        load(3, g).start()
+        return 0
+
+    lax.fori_loop(0, GROUPS, start_key_loads, 0)
 
     @pl.when(head == 0)
     def _():
         def send(g, _):
+            load(0, g).wait()
             far(0, g).start()
+            load(1, g).wait()
             far(1, g).start()
             return 0
 
-        lax.fori_loop(0, GROUPS, send, 0)
+        def drain(g, _):
+            far(0, g).wait_send()
+            far(1, g).wait_send()
+            return 0
+
+        pl.semaphore_wait(barrier, 1)
+        lax.fori_loop(0, LEAD, send, 0)
+
+        @pl.when(core == 1)
+        def _():
+            lax.fori_loop(0, LEAD, drain, 0)
+
+        lax.fori_loop(LEAD, GROUPS, send, 0)
+        lengths_copy.start()
+        lax.fori_loop(0, GROUPS, start_query_loads, 0)
+        lengths_copy.wait()
         bias_a[0:ROWS] = mask_bias(lengths, seq, HALF, 0, ROWS)
         bias_b[...] = mask_bias(lengths, seq, 0, 0, HALF)
 
         def local(g, _):
-            for copy in loads(g):
-                copy.wait()
+            load(2, g).wait()
+            load(3, g).wait()
             for row, keys, bias in ((HALF, ROWS, bias_a), (0, HALF, bias_b)):
                 kk = k_own[0:keys, columns(g)]
                 vv = v_own[0:keys, columns(g)]
@@ -174,23 +198,22 @@
             dk_out[:, columns(g)] = (dk_sum[g] * SCALE + dk_far[g].astype(F32)).astype(BF16)
             return 0
 
-        lax.fori_loop(0, GROUPS, finish, 0)
-
-        def drain(g, _):
-            far(0, g).wait_send()
-            far(1, g).wait_send()
-            return 0
-
-        lax.fori_loop(0, GROUPS, drain, 0)
+        lax.fori_loop(0, GROUPS - 1, finish, 0)
+        lax.fori_loop(jnp.where(core == 1, LEAD, 0), GROUPS, drain, 0)
+        finish(GROUPS - 1, 0)
 
     @pl.when(head == 1)
     def _():
+        lengths_copy.start()
+        lax.fori_loop(0, GROUPS, start_query_loads, 0)
+        pl.semaphore_wait(barrier, 1)
+        lengths_copy.wait()
         bias_a[...] = mask_bias(lengths, seq, ROWS, 0, ROWS + HALF)
         bias_b[...] = mask_bias(lengths, seq, ROWS + HALF, ROWS + HALF, HALF)
 
         def work(g, _):
-            for copy in loads(g):
-                copy.wait()
+            for i in range(4):
+                load(i, g).wait()
             kk = k_own[HALF:ROWS, columns(g)]
             vv = v_own[HALF:ROWS, columns(g)]
             qq = stacked(q_own, HALF, g)
@@ -203,23 +226,55 @@
             put_heads(o_out, HALF, g, dot_nn(vv.T, rounded))
             put_heads(dq_out, HALF, g, dot_nn(kk.T, dscores) * SCALE)
 
-            far(0, g).wait_recv()
-            kk = jnp.concatenate([k_far[g], k_own[0:HALF, columns(g)]], axis=0)
+            k_near = k_own[0:HALF, columns(g)]
+            v_near = v_own[0:HALF, columns(g)]
             qq = stacked(q_own, 0, g)
             gg = stacked(g_own, 0, g)
-            probs = probabilities(kk, qq, bias_a[...])
-            rounded = probs.astype(BF16)
-            dv = dot_nn(rounded, gg).astype(BF16)
-            dv_send[g] = dv[0:ROWS]
+            bias_far, bias_near = bias_a[0:ROWS], bias_a[ROWS:]
+            near_logits = [logits(k_near, qq[part], bias_near) for part in PARTS]
+            near_top = [jnp.max(x, axis=0, keepdims=True) for x in near_logits]
+            near_dprobs = [dot_nt(v_near, gg[part]) for part in PARTS]
+
+            far(0, g).wait_recv()
+            k_there = k_far[g]
+            probs_far, probs_near, near_sum = [], [], []
+            for n, part in enumerate(PARTS):
+                far_logits = logits(k_there, qq[part], bias_far)
+                top = jnp.maximum(near_top[n], jnp.max(far_logits, axis=0, keepdims=True))
+                weights_far = jnp.exp2(far_logits - top)
+                weights_near = jnp.exp2(near_logits[n] - top)
+                total = jnp.sum(weights_far, axis=0, keepdims=True)
+                total += jnp.sum(weights_near, axis=0, keepdims=True)
+                probs_far.append(weights_far * (1.0 / total))
+                probs_near.append(weights_near * (1.0 / total))
+            rounded_far = wide(probs_far)
+            rounded_near = wide(probs_near)
+            dv_send[g] = dot_nn(rounded_far, gg).astype(BF16)
             far(2, g).start()
-            dv_out[0:HALF, columns(g)] = dv[ROWS:]
+            near_sum = [
+                jnp.sum(p * d, axis=0, keepdims=True) for p, d in zip(probs_near, near_dprobs)
+            ]
+
             far(1, g).wait_recv()
-            vv = jnp.concatenate([v_far[g], v_own[0:HALF, columns(g)]], axis=0)
-            dscores = score_gradient(probs, vv, gg)
-            dk = (dot_nn(dscores, qq) * SCALE).astype(BF16)
-            dk_send[g] = dk[0:ROWS]
+            v_there = v_far[g]
+            dscores_far, deltas = [], []
+            for n, part in enumerate(PARTS):
+                dprobs = dot_nt(v_there, gg[part])
+                delta = near_sum[n] + jnp.sum(probs_far[n] * dprobs, axis=0, keepdims=True)
+                dscores_far.append(probs_far[n] * (dprobs - delta))
+                deltas.append(delta)
+            dscores_far = wide(dscores_far)
+            dk_send[g] = (dot_nn(dscores_far, qq) * SCALE).astype(BF16)
             far(3, g).start()
-            dk_out[0:HALF, columns(g)] = dk[ROWS:]
+            dscores_near = wide(
+                [p * (d - delta) for p, d, delta in zip(probs_near, near_dprobs, deltas)]
+            )
+            dv_out[0:HALF, columns(g)] = dot_nn(rounded_near, gg).astype(BF16)
+            dk_out[0:HALF, columns(g)] = (dot_nn(dscores_near, qq) * SCALE).astype(BF16)
+            vv = jnp.concatenate([v_there, v_near], axis=0)
+            kk = jnp.concatenate([k_there, k_near], axis=0)
+            rounded = jnp.concatenate([rounded_far, rounded_near], axis=0)
+            dscores = jnp.concatenate([dscores_far, dscores_near], axis=0)
             put_heads(o_out, 0, g, dot_nn(vv.T, rounded))
             put_heads(dq_out, 0, g, dot_nn(kk.T, dscores) * SCALE)
             return 0

time: 34.8 us -> 34.2 us (0.983)
  Pallas kernels: 34 us -> 33.4 us
    pallas_call x1, Pallas kernels: 31.3 us -> 30.7 us  [body(): pl.pallas_call(kernel, out_shape=[pltpu.VMEM(x.shape, BF16) for x in (que...]
where the time goes in v3:
time: 34.2 us; the launch traced here: 34.1 us
  Pallas kernels  33.4 us (98%)
  between operations  0.64 us (2%)
    pallas_call x1, Pallas kernels, body(): pl.pallas_call(kernel, out_shape=[pltpu.VMEM(x.shape, BF16) for x in (que...  30.7 us
    pallas_call x1, Pallas kernels, body(): pl.pallas_call(store_kernel, out_shape=[jax.ShapeDtypeStruct(x.shape, BF1...  2.71 us

profile of v3, /device:TPU:0, one launch (start us, length us, event | category | flops | bytes accessed | tf_op | source)
XLA Modules:
  0.0 34.1 jit_solution(16802318191642561574)
XLA Ops:
  0.6 30.7 %packed_attention.1 = (bf16[256,5120]{1,0:T(8,128)(2,1)S(1)}, bf16[256,5120]{1,0:T(8,128)(2,1)S(1)}, bf16[256,1024]{1,0:T(8,128)(2,1)S(1)}, bf16[256,1024]{1,0:T(8,128)(2,1)S(1)}) custom-call(s32[16,64]{1,0:T(8,128)} %bitcast.1, bf16[256,5120]{1,0:T(8,128)(2,1)} %q_hbm.1, bf16[256,1024]{1,0:T(8,128)(2,1)} %k_hbm.1, bf16[256,1024]{1,0:T(8,128)(2,1)} %v_hbm.1, ...), custom_call_target="tpu_custom_call" | custom-call | tf_op jit(solution)/shard_map/packed_attention/pallas_call | solution.py:307
  31.4 2.7 %store_results.1 = (bf16[256,5120]{1,0:T(8,128)(2,1)}, bf16[256,5120]{1,0:T(8,128)(2,1)}, bf16[256,1024]{1,0:T(8,128)(2,1)}, bf16[256,1024]{1,0:T(8,128)(2,1)}) custom-call(bf16[256,5120]{1,0:T(8,128)(2,1)S(1)} %get-tuple-element.8.refs_0_, bf16[256,5120]{1,0:T(8,128)(2,1)S(1)} %get-tuple-element.9.refs_1_, bf16[256,1024]{1,0:T(8,128)(2,1)S(1)} %get-tuple-element.10.refs_2_, ...), custom_call_target="tpu_custom_call" | custom-call | tf_op jit(solution)/shard_map/store_results/pallas_call | solution.py:330

commit v4 on v2

--- a/solution.py
+++ b/solution.py
@@ -46,9 +46,13 @@
     return pl.ds(pl.multiple_of(group * WIDTH, WIDTH), WIDTH)
 
 
+def logits(keys, queries, bias):
+    return dot_nt(keys, queries) * TO_EXP2 + jnp.concatenate([bias] * RATIO, axis=1)
+
+
 def probabilities(keys, queries, bias):
-    logits = dot_nt(keys, queries) * TO_EXP2 + jnp.concatenate([bias] * RATIO, axis=1)
-    weights = jnp.exp2(logits - jnp.max(logits, axis=0, keepdims=True))
+    scaled = logits(keys, queries, bias)
+    weights = jnp.exp2(scaled - jnp.max(scaled, axis=0, keepdims=True))
     return weights * (1.0 / jnp.sum(weights, axis=0, keepdims=True))
 
 
@@ -80,71 +84,73 @@
     lengths_hbm, q_hbm, k_hbm, v_hbm, g_hbm,
     o_out, dq_out, dk_out, dv_out,
     q_own, k_own, v_own, g_own,
-    k_far, v_far, dk_send, dv_send, dk_far, dv_far, dk_sum, dv_sum,
-    bias_a, bias_b, lengths, lengths_sem, load_sem, send_sem, recv_sem,
+    kv_far, dkv_send, dkv_far, dk_sum, dv_sum,
+    bias_a, bias_b, lengths, load_sem, send_sem, recv_sem,
 ):
     seq = lax.axis_index("seq")
     head = lax.axis_index("head")
+    core = lax.rem(seq, 2)
     partner = (seq, 1 - head)
     barrier = pltpu.get_barrier_semaphore()
     pl.semaphore_signal(barrier, inc=1, device_id=partner, device_id_type=MESH)
 
-    lengths_copy = pltpu.make_async_copy(lengths_hbm, lengths, lengths_sem)
-    lengths_copy.start()
-
-    def loads(g):
-        wide = pl.ds(pl.multiple_of(g * WIDE, WIDTH), WIDE)
-        return [
-            pltpu.make_async_copy(src.at[:, where], dst.at[:, where], load_sem.at[i, g])
-            for i, (src, dst, where) in enumerate(
-                (
-                    (k_hbm, k_own, columns(g)),
-                    (q_hbm, q_own, wide),
-                    (g_hbm, g_own, wide),
-                    (v_hbm, v_own, columns(g)),
-                )
-            )
-        ]
-
-    def far(i, g):
+    def load(i):
         src, dst = (
-            (k_hbm.at[:, columns(g)], k_far.at[g]),
-            (v_hbm.at[:, columns(g)], v_far.at[g]),
-            (dv_send.at[g], dv_far.at[g]),
-            (dk_send.at[g], dk_far.at[g]),
+            (k_hbm, k_own), (v_hbm, v_own), (q_hbm, q_own), (g_hbm, g_own), (lengths_hbm, lengths)
         )[i]
+        return pltpu.make_async_copy(src, dst, load_sem.at[i])
+
+    def send(src, dst, sent, landed):
         return pltpu.make_async_remote_copy(
             src_ref=src,
             dst_ref=dst,
-            send_sem=send_sem.at[i, g],
-            recv_sem=recv_sem.at[i, g],
+            send_sem=send_sem.at[sent],
+            recv_sem=recv_sem.at[landed],
             device_id=partner,
             device_id_type=MESH,
         )
 
-    def start_loads(g, _):
-        for copy in loads(g):
-            copy.start()
-        return 0
-
-    lax.fori_loop(0, GROUPS, start_loads, 0)
-    lengths_copy.wait()
-    pl.semaphore_wait(barrier, 1)
+    def far(i, g, sent=1):
+        at = 2 * g + i % 2
+        if i < 2:
+            return send((k_own, v_own)[i].at[:, columns(g)], kv_far.at[at], sent, at)
+        return send(dkv_send.at[at], dkv_far.at[at], sent, at)
+
+    def wait_sent(sent, blocks):
+        every = kv_far.at[0:blocks]
+        send(every, every, sent, 0).wait_send()
+
+    load(0).start()
+    load(1).start()
 
     @pl.when(head == 0)
     def _():
-        def send(g, _):
+        pl.semaphore_wait(barrier, 1)
+        load(0).wait()
+        far(0, 0, 0).start()
+        load(1).wait()
+        far(1, 0, 0).start()
+
+        @pl.when(core == 1)
+        def _():
+            wait_sent(0, 2)
+
+        def send_group(g, _):
             far(0, g).start()
             far(1, g).start()
             return 0
 
-        lax.fori_loop(0, GROUPS, send, 0)
+        lax.fori_loop(1, GROUPS, send_group, 0)
+        load(4).start()
+        load(2).start()
+        load(3).start()
+        load(4).wait()
         bias_a[0:ROWS] = mask_bias(lengths, seq, HALF, 0, ROWS)
         bias_b[...] = mask_bias(lengths, seq, 0, 0, HALF)
+        load(2).wait()
+        load(3).wait()
 
         def local(g, _):
-            for copy in loads(g):
-                copy.wait()
             for row, keys, bias in ((HALF, ROWS, bias_a), (0, HALF, bias_b)):
                 kk = k_own[0:keys, columns(g)]
                 vv = v_own[0:keys, columns(g)]
@@ -169,28 +175,33 @@
 
         def finish(g, _):
             far(2, g).wait_recv()
-            dv_out[:, columns(g)] = (dv_sum[g] + dv_far[g].astype(F32)).astype(BF16)
+            dv_out[:, columns(g)] = (dv_sum[g] + dkv_far[2 * g].astype(F32)).astype(BF16)
             far(3, g).wait_recv()
-            dk_out[:, columns(g)] = (dk_sum[g] * SCALE + dk_far[g].astype(F32)).astype(BF16)
+            dk_out[:, columns(g)] = (dk_sum[g] * SCALE + dkv_far[2 * g + 1].astype(F32)).astype(BF16)
             return 0
 
-        lax.fori_loop(0, GROUPS, finish, 0)
-
-        def drain(g, _):
-            far(0, g).wait_send()
-            far(1, g).wait_send()
-            return 0
-
-        lax.fori_loop(0, GROUPS, drain, 0)
+        lax.fori_loop(0, GROUPS - 1, finish, 0)
+
+        @pl.when(core == 0)
+        def _():
+            wait_sent(0, 2)
+
+        wait_sent(1, 2 * GROUPS - 2)
+        finish(GROUPS - 1, 0)
 
     @pl.when(head == 1)
     def _():
+        load(4).start()
+        load(2).start()
+        load(3).start()
+        pl.semaphore_wait(barrier, 1)
+        load(4).wait()
         bias_a[...] = mask_bias(lengths, seq, ROWS, 0, ROWS + HALF)
         bias_b[...] = mask_bias(lengths, seq, ROWS + HALF, ROWS + HALF, HALF)
+        for i in range(4):
+            load(i).wait()
 
         def work(g, _):
-            for copy in loads(g):
-                copy.wait()
             kk = k_own[HALF:ROWS, columns(g)]
             vv = v_own[HALF:ROWS, columns(g)]
             qq = stacked(q_own, HALF, g)
@@ -203,35 +214,51 @@
             put_heads(o_out, HALF, g, dot_nn(vv.T, rounded))
             put_heads(dq_out, HALF, g, dot_nn(kk.T, dscores) * SCALE)
 
-            far(0, g).wait_recv()
-            kk = jnp.concatenate([k_far[g], k_own[0:HALF, columns(g)]], axis=0)
+            k_near = k_own[0:HALF, columns(g)]
+            v_near = v_own[0:HALF, columns(g)]
             qq = stacked(q_own, 0, g)
             gg = stacked(g_own, 0, g)
-            probs = probabilities(kk, qq, bias_a[...])
-            rounded = probs.astype(BF16)
-            dv = dot_nn(rounded, gg).astype(BF16)
-            dv_send[g] = dv[0:ROWS]
+            near_logits = logits(k_near, qq, bias_a[ROWS:])
+            near_top = jnp.max(near_logits, axis=0, keepdims=True)
+            near_dprobs = dot_nt(v_near, gg)
+
+            far(0, g).wait_recv()
+            k_there = kv_far[2 * g]
+            far_logits = logits(k_there, qq, bias_a[0:ROWS])
+            top = jnp.maximum(near_top, jnp.max(far_logits, axis=0, keepdims=True))
+            probs_far = jnp.exp2(far_logits - top)
+            probs_near = jnp.exp2(near_logits - top)
+            total = jnp.sum(probs_far, axis=0, keepdims=True)
+            total += jnp.sum(probs_near, axis=0, keepdims=True)
+            probs_far *= 1.0 / total
+            probs_near *= 1.0 / total
+            rounded_far = probs_far.astype(BF16)
+            rounded_near = probs_near.astype(BF16)
+            dkv_send[2 * g] = dot_nn(rounded_far, gg).astype(BF16)
             far(2, g).start()
-            dv_out[0:HALF, columns(g)] = dv[ROWS:]
+            near_sum = jnp.sum(probs_near * near_dprobs, axis=0, keepdims=True)
+
             far(1, g).wait_recv()
-            vv = jnp.concatenate([v_far[g], v_own[0:HALF, columns(g)]], axis=0)
-            dscores = score_gradient(probs, vv, gg)
-            dk = (dot_nn(dscores, qq) * SCALE).astype(BF16)
-            dk_send[g] = dk[0:ROWS]
+            v_there = kv_far[2 * g + 1]
+            dprobs = dot_nt(v_there, gg)
+            delta = near_sum + jnp.sum(probs_far * dprobs, axis=0, keepdims=True)
+            dscores_far = (probs_far * (dprobs - delta)).astype(BF16)
+            dkv_send[2 * g + 1] = (dot_nn(dscores_far, qq) * SCALE).astype(BF16)
             far(3, g).start()
-            dk_out[0:HALF, columns(g)] = dk[ROWS:]
+            dscores_near = (probs_near * (near_dprobs - delta)).astype(BF16)
+            dv_out[0:HALF, columns(g)] = dot_nn(rounded_near, gg).astype(BF16)
+            dk_out[0:HALF, columns(g)] = (dot_nn(dscores_near, qq) * SCALE).astype(BF16)
+            vv = jnp.concatenate([v_there, v_near], axis=0)
+            kk = jnp.concatenate([k_there, k_near], axis=0)
+            rounded = jnp.concatenate([rounded_far, rounded_near], axis=0)
+            dscores = jnp.concatenate([dscores_far, dscores_near], axis=0)
             put_heads(o_out, 0, g, dot_nn(vv.T, rounded))
             put_heads(dq_out, 0, g, dot_nn(kk.T, dscores) * SCALE)
             return 0
 
         lax.fori_loop(0, GROUPS, work, 0)
 
-        def drain(g, _):
-            far(2, g).wait_send()
-            far(3, g).wait_send()
-            return 0
-
-        lax.fori_loop(0, GROUPS, drain, 0)
+        wait_sent(1, 2 * GROUPS)
 
 
 def store_kernel(*refs):
@@ -247,7 +274,7 @@
 
 def body(queries, keys, values, output_gradient, document_lengths):
     hbm = pl.BlockSpec(memory_space=pl.ANY)
-    block = pltpu.VMEM((GROUPS, ROWS, WIDTH), BF16)
+    blocks = pltpu.VMEM((2 * GROUPS, ROWS, WIDTH), BF16)
     total = pltpu.VMEM((GROUPS, ROWS, WIDTH), F32)
     results = pl.pallas_call(
         kernel,
@@ -258,14 +285,13 @@
             pltpu.VMEM(keys.shape, BF16),
             pltpu.VMEM(values.shape, BF16),
             pltpu.VMEM(queries.shape, BF16),
-            block, block, block, block, block, block, total, total,
+            blocks, blocks, blocks, total, total,
             pltpu.VMEM((ROWS + HALF, HALF), F32),
             pltpu.VMEM((HALF, HALF), F32),
             pltpu.SMEM(document_lengths.shape[::-1], jnp.int32),
-            pltpu.SemaphoreType.DMA,
-            pltpu.SemaphoreType.DMA((4, GROUPS)),
-            pltpu.SemaphoreType.DMA((4, GROUPS)),
-            pltpu.SemaphoreType.DMA((4, GROUPS)),
+            pltpu.SemaphoreType.DMA((5,)),
+            pltpu.SemaphoreType.DMA((2,)),
+            pltpu.SemaphoreType.DMA((2 * GROUPS,)),
         ],
         compiler_params=pltpu.CompilerParams(
             collective_id=0, has_side_effects=True, vmem_limit_bytes=54 << 20

time: 34.8 us -> 33.5 us (0.963)
  Pallas kernels: 34 us -> 32.8 us
    pallas_call x1, Pallas kernels: 31.3 us -> 30 us  [body(): pl.pallas_call(kernel, out_shape=[pltpu.VMEM(x.shape, BF16) for x in (que...]
where the time goes in v4:
time: 33.5 us; the launch traced here: 33.4 us
  Pallas kernels  32.8 us (98%)
  between operations  0.64 us (2%)
    pallas_call x1, Pallas kernels, body(): pl.pallas_call(kernel, out_shape=[pltpu.VMEM(x.shape, BF16) for x in (que...  30 us
    pallas_call x1, Pallas kernels, body(): pl.pallas_call(store_kernel, out_shape=[jax.ShapeDtypeStruct(x.shape, BF1...  2.71 us

profile of v4, /device:TPU:0, one launch (start us, length us, event | category | flops | bytes accessed | tf_op | source)
XLA Modules:
  0.0 33.4 jit_solution(3777895074945747351)
XLA Ops:
  0.6 30.0 %packed_attention.1 = (bf16[256,5120]{1,0:T(8,128)(2,1)S(1)}, bf16[256,5120]{1,0:T(8,128)(2,1)S(1)}, bf16[256,1024]{1,0:T(8,128)(2,1)S(1)}, bf16[256,1024]{1,0:T(8,128)(2,1)S(1)}) custom-call(s32[16,64]{1,0:T(8,128)} %bitcast.1, bf16[256,5120]{1,0:T(8,128)(2,1)} %q_hbm.1, bf16[256,1024]{1,0:T(8,128)(2,1)} %k_hbm.1, bf16[256,1024]{1,0:T(8,128)(2,1)} %v_hbm.1, ...), custom_call_target="tpu_custom_call" | custom-call | tf_op jit(solution)/shard_map/packed_attention/pallas_call | solution.py:279
  30.7 2.7 %store_results.1 = (bf16[256,5120]{1,0:T(8,128)(2,1)}, bf16[256,5120]{1,0:T(8,128)(2,1)}, bf16[256,1024]{1,0:T(8,128)(2,1)}, bf16[256,1024]{1,0:T(8,128)(2,1)}) custom-call(bf16[256,5120]{1,0:T(8,128)(2,1)S(1)} %get-tuple-element.8.refs_0_, bf16[256,5120]{1,0:T(8,128)(2,1)S(1)} %get-tuple-element.9.refs_1_, bf16[256,1024]{1,0:T(8,128)(2,1)S(1)} %get-tuple-element.10.refs_2_, ...), custom_call_target="tpu_custom_call" | custom-call | tf_op jit(solution)/shard_map/store_results/pallas_call | solution.py:301

commit v5 on v4

--- a/solution.py
+++ b/solution.py
@@ -35,7 +35,7 @@
 def stacked(ref, row, group):
     return jnp.concatenate(
         [
-            ref[pl.ds(row, HALF), pl.ds(pl.multiple_of(group * WIDE + h * WIDTH, WIDTH), WIDTH)]
+            ref[pl.ds(row, HALF), columns(group * RATIO + h)]
             for h in range(RATIO)
         ],
         axis=0,
@@ -43,6 +43,8 @@
 
 
 def columns(group):
+    if isinstance(group, int):
+        return slice(group * WIDTH, (group + 1) * WIDTH)
     return pl.ds(pl.multiple_of(group * WIDTH, WIDTH), WIDTH)
 
 
@@ -65,8 +67,7 @@
 def put_heads(ref, row, group, transposed):
     for h in range(RATIO):
         block = transposed[:, h * WIDTH : (h + 1) * WIDTH].T
-        where = pl.ds(pl.multiple_of(group * WIDE + h * WIDTH, WIDTH), WIDTH)
-        ref[pl.ds(row, HALF), where] = block.astype(BF16)
+        ref[pl.ds(row, HALF), columns(group * RATIO + h)] = block.astype(BF16)
 
 
 def mask_bias(lengths, block, first_query, first_key, keys):
@@ -85,11 +86,14 @@
     o_out, dq_out, dk_out, dv_out,
     q_own, k_own, v_own, g_own,
     kv_far, dkv_send, dkv_far, dk_sum, dv_sum,
-    bias_a, bias_b, lengths, load_sem, send_sem, recv_sem,
+    lent_wide, lent, given_wide, given,
+    bias_a, bias_b, bias_lent, lengths, load_sem, send_sem, recv_sem,
 ):
     seq = lax.axis_index("seq")
     head = lax.axis_index("head")
     core = lax.rem(seq, 2)
+    last = GROUPS - 1
+    groups = jnp.where(core == 0, last, GROUPS)
     partner = (seq, 1 - head)
     barrier = pltpu.get_barrier_semaphore()
     pl.semaphore_signal(barrier, inc=1, device_id=partner, device_id_type=MESH)
@@ -116,6 +120,16 @@
             return send((k_own, v_own)[i].at[:, columns(g)], kv_far.at[at], sent, at)
         return send(dkv_send.at[at], dkv_far.at[at], sent, at)
 
+    def lend(i):
+        rows, wide, narrow = slice(0, HALF), slice(last * WIDE, GROUPS * WIDE), columns(last)
+        src = (q_hbm.at[rows, wide], g_hbm.at[rows, wide], k_hbm.at[rows, narrow], v_hbm.at[rows, narrow])
+        dst = (lent_wide if i < 2 else lent).at[i % 2]
+        return send(src[i], dst, 0, 2 * GROUPS - 2 + i)
+
+    def give_back(i):
+        src, dst = (given_wide, lent_wide) if i < 2 else (given, lent)
+        return send(src.at[i % 2], dst.at[i % 2], 0, 2 * GROUPS - 2 + i)
+
     def wait_sent(sent, blocks):
         every = kv_far.at[0:blocks]
         send(every, every, sent, 0).wait_send()
@@ -140,7 +154,7 @@
             far(1, g).start()
             return 0
 
-        lax.fori_loop(1, GROUPS, send_group, 0)
+        lax.fori_loop(1, groups, send_group, 0)
         load(4).start()
         load(2).start()
         load(3).start()
@@ -180,14 +194,38 @@
             dk_out[:, columns(g)] = (dk_sum[g] * SCALE + dkv_far[2 * g + 1].astype(F32)).astype(BF16)
             return 0
 
-        lax.fori_loop(0, GROUPS - 1, finish, 0)
-
         @pl.when(core == 0)
         def _():
+            bias_lent[...] = mask_bias(lengths, seq, ROWS, 0, ROWS + HALF)
+            for i in range(4):
+                lend(i).wait_recv()
+            kk = jnp.concatenate([k_own[:, columns(last)], lent[0]], axis=0)
+            vv = jnp.concatenate([v_own[:, columns(last)], lent[1]], axis=0)
+            qq = stacked(lent_wide.at[0], 0, 0)
+            gg = stacked(lent_wide.at[1], 0, 0)
+            probs = probabilities(kk, qq, bias_lent[...])
+            rounded = probs.astype(BF16)
+            dscores = score_gradient(probs, vv, gg)
+            dv = dot_nn(rounded, gg)
+            dk = dot_nn(dscores, qq) * SCALE
+            dv_out[:, columns(last)] = (dv_sum[last] + dv[0:ROWS]).astype(BF16)
+            dk_out[:, columns(last)] = (dk_sum[last] * SCALE + dk[0:ROWS]).astype(BF16)
+            given[0] = dk[ROWS:].astype(BF16)
+            given[1] = dv[ROWS:].astype(BF16)
+            put_heads(given_wide.at[0], 0, 0, dot_nn(vv.T, rounded))
+            put_heads(given_wide.at[1], 0, 0, dot_nn(kk.T, dscores) * SCALE)
             wait_sent(0, 2)
-
-        wait_sent(1, 2 * GROUPS - 2)
-        finish(GROUPS - 1, 0)
+            wait_sent(1, 2 * GROUPS - 4)
+            for i in range(4):
+                give_back(i).start()
+            lax.fori_loop(0, last, finish, 0)
+            wait_sent(0, 6)
+
+        @pl.when(core == 1)
+        def _():
+            lax.fori_loop(0, last, finish, 0)
+            wait_sent(1, 2 * GROUPS - 2)
+            finish(last, 0)
 
     @pl.when(head == 1)
     def _():
@@ -195,13 +233,19 @@
         load(2).start()
         load(3).start()
         pl.semaphore_wait(barrier, 1)
+
+        @pl.when(core == 0)
+        def _():
+            for i in range(4):
+                lend(i).start()
+
         load(4).wait()
         bias_a[...] = mask_bias(lengths, seq, ROWS, 0, ROWS + HALF)
         bias_b[...] = mask_bias(lengths, seq, ROWS + HALF, ROWS + HALF, HALF)
         for i in range(4):
             load(i).wait()
 
-        def work(g, _):
+        def work_near(g):
             kk = k_own[HALF:ROWS, columns(g)]
             vv = v_own[HALF:ROWS, columns(g)]
             qq = stacked(q_own, HALF, g)
@@ -214,6 +258,8 @@
             put_heads(o_out, HALF, g, dot_nn(vv.T, rounded))
             put_heads(dq_out, HALF, g, dot_nn(kk.T, dscores) * SCALE)
 
+        def work(g, _):
+            work_near(g)
             k_near = k_own[0:HALF, columns(g)]
             v_near = v_own[0:HALF, columns(g)]
             qq = stacked(q_own, 0, g)
@@ -256,9 +302,24 @@
             put_heads(dq_out, 0, g, dot_nn(kk.T, dscores) * SCALE)
             return 0
 
-        lax.fori_loop(0, GROUPS, work, 0)
-
-        wait_sent(1, 2 * GROUPS)
+        lax.fori_loop(0, groups, work, 0)
+
+        @pl.when(core == 0)
+        def _():
+            work_near(last)
+            wait_sent(0, 6)
+            wait_sent(1, 2 * GROUPS - 2)
+            for i in range(4):
+                give_back(i).wait_recv()
+            wide = slice(last * WIDE, GROUPS * WIDE)
+            o_out[0:HALF, wide] = lent_wide[0]
+            dq_out[0:HALF, wide] = lent_wide[1]
+            dk_out[0:HALF, columns(last)] = lent[0]
+            dv_out[0:HALF, columns(last)] = lent[1]
+
+        @pl.when(core == 1)
+        def _():
+            wait_sent(1, 2 * GROUPS)
 
 
 def store_kernel(*refs):
@@ -286,12 +347,17 @@
             pltpu.VMEM(values.shape, BF16),
             pltpu.VMEM(queries.shape, BF16),
             blocks, blocks, blocks, total, total,
+            pltpu.VMEM((2, HALF, WIDE), BF16),
+            pltpu.VMEM((2, HALF, WIDTH), BF16),
+            pltpu.VMEM((2, HALF, WIDE), BF16),
+            pltpu.VMEM((2, HALF, WIDTH), BF16),
             pltpu.VMEM((ROWS + HALF, HALF), F32),
             pltpu.VMEM((HALF, HALF), F32),
+            pltpu.VMEM((ROWS + HALF, HALF), F32),
             pltpu.SMEM(document_lengths.shape[::-1], jnp.int32),
             pltpu.SemaphoreType.DMA((5,)),
             pltpu.SemaphoreType.DMA((2,)),
-            pltpu.SemaphoreType.DMA((2 * GROUPS,)),
+            pltpu.SemaphoreType.DMA((2 * GROUPS + 2,)),
         ],
         compiler_params=pltpu.CompilerParams(
             collective_id=0, has_side_effects=True, vmem_limit_bytes=54 << 20

time: 33.5 us -> 33.9 us (1.012)
  the two profiles are of different devices: /device:TPU:0 before, /device:TPU:1 now
where the time goes in v5:
time: 33.9 us; the launch traced here: 33.7 us
  Pallas kernels  33.1 us (98%)
  between operations  0.64 us (2%)
    pallas_call x1, Pallas kernels, body(): pl.pallas_call(kernel, out_shape=[pltpu.VMEM(x.shape, BF16) for x in (que...  30.4 us
    pallas_call x1, Pallas kernels, body(): pl.pallas_call(store_kernel, out_shape=[jax.ShapeDtypeStruct(x.shape, BF1...  2.71 us

profile of v5, /device:TPU:1, one launch (start us, length us, event | category | flops | bytes accessed | tf_op | source)
XLA Modules:
  0.0 33.7 jit_solution(7248805864097476202)
XLA Ops:
  0.6 30.4 %packed_attention.1 = (bf16[256,5120]{1,0:T(8,128)(2,1)S(1)}, bf16[256,5120]{1,0:T(8,128)(2,1)S(1)}, bf16[256,1024]{1,0:T(8,128)(2,1)S(1)}, bf16[256,1024]{1,0:T(8,128)(2,1)S(1)}) custom-call(s32[16,64]{1,0:T(8,128)} %bitcast.1, bf16[256,5120]{1,0:T(8,128)(2,1)} %q_hbm.1, bf16[256,1024]{1,0:T(8,128)(2,1)} %k_hbm.1, bf16[256,1024]{1,0:T(8,128)(2,1)} %v_hbm.1, ...), custom_call_target="tpu_custom_call" | custom-call | tf_op jit(solution)/shard_map/packed_attention/pallas_call | solution.py:340
  31.0 2.7 %store_results.1 = (bf16[256,5120]{1,0:T(8,128)(2,1)}, bf16[256,5120]{1,0:T(8,128)(2,1)}, bf16[256,1024]{1,0:T(8,128)(2,1)}, bf16[256,1024]{1,0:T(8,128)(2,1)}) custom-call(bf16[256,5120]{1,0:T(8,128)(2,1)S(1)} %get-tuple-element.8.refs_0_, bf16[256,5120]{1,0:T(8,128)(2,1)S(1)} %get-tuple-element.9.refs_1_, bf16[256,1024]{1,0:T(8,128)(2,1)S(1)} %get-tuple-element.10.refs_2_, ...), custom_call_target="tpu_custom_call" | custom-call | tf_op jit(solution)/shard_map/store_results/pallas_call | solution.py:367

commit v6 on v5

--- a/solution.py
+++ b/solution.py
@@ -93,7 +93,7 @@
     head = lax.axis_index("head")
     core = lax.rem(seq, 2)
     last = GROUPS - 1
-    groups = jnp.where(core == 0, last, GROUPS)
+    groups = jnp.where(core == 1, last, GROUPS)
     partner = (seq, 1 - head)
     barrier = pltpu.get_barrier_semaphore()
     pl.semaphore_signal(barrier, inc=1, device_id=partner, device_id_type=MESH)
@@ -154,7 +154,13 @@
             far(1, g).start()
             return 0
 
-        lax.fori_loop(1, groups, send_group, 0)
+        lax.fori_loop(1, 2, send_group, 0)
+
+        @pl.when(core == 1)
+        def _():
+            wait_sent(1, 2)
+
+        lax.fori_loop(2, groups, send_group, 0)
         load(4).start()
         load(2).start()
         load(3).start()
@@ -194,7 +200,7 @@
             dk_out[:, columns(g)] = (dk_sum[g] * SCALE + dkv_far[2 * g + 1].astype(F32)).astype(BF16)
             return 0
 
-        @pl.when(core == 0)
+        @pl.when(core == 1)
         def _():
             bias_lent[...] = mask_bias(lengths, seq, ROWS, 0, ROWS + HALF)
             for i in range(4):
@@ -214,16 +220,17 @@
             given[1] = dv[ROWS:].astype(BF16)
             put_heads(given_wide.at[0], 0, 0, dot_nn(vv.T, rounded))
             put_heads(given_wide.at[1], 0, 0, dot_nn(kk.T, dscores) * SCALE)
-            wait_sent(0, 2)
-            wait_sent(1, 2 * GROUPS - 4)
+            wait_sent(1, 2 * GROUPS - 6)
+            lax.fori_loop(0, 0, finish, 0)
             for i in range(4):
                 give_back(i).start()
             lax.fori_loop(0, last, finish, 0)
             wait_sent(0, 6)
 
-        @pl.when(core == 1)
+        @pl.when(core == 0)
         def _():
             lax.fori_loop(0, last, finish, 0)
+            wait_sent(0, 2)
             wait_sent(1, 2 * GROUPS - 2)
             finish(last, 0)
 
@@ -234,7 +241,7 @@
         load(3).start()
         pl.semaphore_wait(barrier, 1)
 
-        @pl.when(core == 0)
+        @pl.when(core == 1)
         def _():
             for i in range(4):
                 lend(i).start()
@@ -304,7 +311,7 @@
 
         lax.fori_loop(0, groups, work, 0)
 
-        @pl.when(core == 0)
+        @pl.when(core == 1)
         def _():
             work_near(last)
             wait_sent(0, 6)
@@ -317,7 +324,7 @@
             dk_out[0:HALF, columns(last)] = lent[0]
             dv_out[0:HALF, columns(last)] = lent[1]
 
-        @pl.when(core == 1)
+        @pl.when(core == 0)
         def _():
             wait_sent(1, 2 * GROUPS)
 

time: 33.9 us -> 32.7 us (0.965)
  the two profiles are of different devices: /device:TPU:1 before, /device:TPU:0 now
where the time goes in v6:
time: 32.7 us; the launch traced here: 32.5 us
  Pallas kernels  31.9 us (98%)
  between operations  0.64 us (2%)
    pallas_call x1, Pallas kernels, body(): pl.pallas_call(kernel, out_shape=[pltpu.VMEM(x.shape, BF16) for x in (que...  29.2 us
    pallas_call x1, Pallas kernels, body(): pl.pallas_call(store_kernel, out_shape=[jax.ShapeDtypeStruct(x.shape, BF1...  2.71 us

profile of v6, /device:TPU:0, one launch (start us, length us, event | category | flops | bytes accessed | tf_op | source)
XLA Modules:
  0.0 32.5 jit_solution(6904336376369363229)
XLA Ops:
  0.6 29.2 %packed_attention.1 = (bf16[256,5120]{1,0:T(8,128)(2,1)S(1)}, bf16[256,5120]{1,0:T(8,128)(2,1)S(1)}, bf16[256,1024]{1,0:T(8,128)(2,1)S(1)}, bf16[256,1024]{1,0:T(8,128)(2,1)S(1)}) custom-call(s32[16,64]{1,0:T(8,128)} %bitcast.1, bf16[256,5120]{1,0:T(8,128)(2,1)} %q_hbm.1, bf16[256,1024]{1,0:T(8,128)(2,1)} %k_hbm.1, bf16[256,1024]{1,0:T(8,128)(2,1)} %v_hbm.1, ...), custom_call_target="tpu_custom_call" | custom-call | tf_op jit(solution)/shard_map/packed_attention/pallas_call | solution.py:347
  29.8 2.7 %store_results.1 = (bf16[256,5120]{1,0:T(8,128)(2,1)}, bf16[256,5120]{1,0:T(8,128)(2,1)}, bf16[256,1024]{1,0:T(8,128)(2,1)}, bf16[256,1024]{1,0:T(8,128)(2,1)}) custom-call(bf16[256,5120]{1,0:T(8,128)(2,1)S(1)} %get-tuple-element.8.refs_0_, bf16[256,5120]{1,0:T(8,128)(2,1)S(1)} %get-tuple-element.9.refs_1_, bf16[256,1024]{1,0:T(8,128)(2,1)S(1)} %get-tuple-element.10.refs_2_, ...), custom_call_target="tpu_custom_call" | custom-call | tf_op jit(solution)/shard_map/store_results/pallas_call | solution.py:374

commit v7 on v6

--- a/solution.py
+++ b/solution.py
@@ -28,6 +28,10 @@
     return lax.dot_general(a, b, (((1,), (1,)), ((), ())), preferred_element_type=F32)
 
 
+def dot_tn(a, b):
+    return lax.dot_general(a, b, (((0,), (0,)), ((), ())), preferred_element_type=F32)
+
+
 def dot_nn(a, b):
     return jnp.dot(a, b, preferred_element_type=F32)
 
@@ -66,7 +70,7 @@
 
 def put_heads(ref, row, group, transposed):
     for h in range(RATIO):
-        block = transposed[:, h * WIDTH : (h + 1) * WIDTH].T
+        block = transposed[h * WIDTH : (h + 1) * WIDTH]
         ref[pl.ds(row, HALF), columns(group * RATIO + h)] = block.astype(BF16)
 
 
@@ -124,11 +128,15 @@
         rows, wide, narrow = slice(0, HALF), slice(last * WIDE, GROUPS * WIDE), columns(last)
         src = (q_hbm.at[rows, wide], g_hbm.at[rows, wide], k_hbm.at[rows, narrow], v_hbm.at[rows, narrow])
         dst = (lent_wide if i < 2 else lent).at[i % 2]
-        return send(src[i], dst, 0, 2 * GROUPS - 2 + i)
+        return send(src[i], dst, 0, 2 * GROUPS - 2 + i // 2)
 
     def give_back(i):
         src, dst = (given_wide, lent_wide) if i < 2 else (given, lent)
-        return send(src.at[i % 2], dst.at[i % 2], 0, 2 * GROUPS - 2 + i)
+        return send(src.at[i % 2], dst.at[i % 2], 0, 2 * GROUPS - 2 + i // 2)
+
+    def wait_lent():
+        send(lent_wide, lent_wide, 0, 2 * GROUPS - 2).wait_recv()
+        send(lent, lent, 0, 2 * GROUPS - 1).wait_recv()
 
     def wait_sent(sent, blocks):
         every = kv_far.at[0:blocks]
@@ -187,8 +195,8 @@
                 else:
                     dv_sum[g, 0:HALF] += dv
                     dk_sum[g, 0:HALF] += dk
-                put_heads(o_out, row, g, dot_nn(vv.T, rounded))
-                put_heads(dq_out, row, g, dot_nn(kk.T, dscores) * SCALE)
+                put_heads(o_out, row, g, dot_tn(rounded, vv))
+                put_heads(dq_out, row, g, dot_tn(dscores, kk) * SCALE)
             return 0
 
         lax.fori_loop(0, GROUPS, local, 0)
@@ -203,8 +211,7 @@
         @pl.when(core == 1)
         def _():
             bias_lent[...] = mask_bias(lengths, seq, ROWS, 0, ROWS + HALF)
-            for i in range(4):
-                lend(i).wait_recv()
+            wait_lent()
             kk = jnp.concatenate([k_own[:, columns(last)], lent[0]], axis=0)
             vv = jnp.concatenate([v_own[:, columns(last)], lent[1]], axis=0)
             qq = stacked(lent_wide.at[0], 0, 0)
@@ -218,8 +225,8 @@
             dk_out[:, columns(last)] = (dk_sum[last] * SCALE + dk[0:ROWS]).astype(BF16)
             given[0] = dk[ROWS:].astype(BF16)
             given[1] = dv[ROWS:].astype(BF16)
-            put_heads(given_wide.at[0], 0, 0, dot_nn(vv.T, rounded))
-            put_heads(given_wide.at[1], 0, 0, dot_nn(kk.T, dscores) * SCALE)
+            put_heads(given_wide.at[0], 0, 0, dot_tn(rounded, vv))
+            put_heads(given_wide.at[1], 0, 0, dot_tn(dscores, kk) * SCALE)
             wait_sent(1, 2 * GROUPS - 6)
             lax.fori_loop(0, 0, finish, 0)
             for i in range(4):
@@ -262,8 +269,8 @@
             dscores = score_gradient(probs, vv, gg)
             dv_out[HALF:ROWS, columns(g)] = dot_nn(rounded, gg).astype(BF16)
             dk_out[HALF:ROWS, columns(g)] = (dot_nn(dscores, qq) * SCALE).astype(BF16)
-            put_heads(o_out, HALF, g, dot_nn(vv.T, rounded))
-            put_heads(dq_out, HALF, g, dot_nn(kk.T, dscores) * SCALE)
+            put_heads(o_out, HALF, g, dot_tn(rounded, vv))
+            put_heads(dq_out, HALF, g, dot_tn(dscores, kk) * SCALE)
 
         def work(g, _):
             work_near(g)
@@ -305,8 +312,8 @@
             kk = jnp.concatenate([k_there, k_near], axis=0)
             rounded = jnp.concatenate([rounded_far, rounded_near], axis=0)
             dscores = jnp.concatenate([dscores_far, dscores_near], axis=0)
-            put_heads(o_out, 0, g, dot_nn(vv.T, rounded))
-            put_heads(dq_out, 0, g, dot_nn(kk.T, dscores) * SCALE)
+            put_heads(o_out, 0, g, dot_tn(rounded, vv))
+            put_heads(dq_out, 0, g, dot_tn(dscores, kk) * SCALE)
             return 0
 
         lax.fori_loop(0, groups, work, 0)
@@ -316,8 +323,7 @@
             work_near(last)
             wait_sent(0, 6)
             wait_sent(1, 2 * GROUPS - 2)
-            for i in range(4):
-                give_back(i).wait_recv()
+            wait_lent()
             wide = slice(last * WIDE, GROUPS * WIDE)
             o_out[0:HALF, wide] = lent_wide[0]
             dq_out[0:HALF, wide] = lent_wide[1]
@@ -364,7 +370,7 @@
             pltpu.SMEM(document_lengths.shape[::-1], jnp.int32),
             pltpu.SemaphoreType.DMA((5,)),
             pltpu.SemaphoreType.DMA((2,)),
-            pltpu.SemaphoreType.DMA((2 * GROUPS + 2,)),
+            pltpu.SemaphoreType.DMA((2 * GROUPS,)),
         ],
         compiler_params=pltpu.CompilerParams(
             collective_id=0, has_side_effects=True, vmem_limit_bytes=54 << 20

time: 32.7 us -> 32.6 us (level)
  no operation moved by 1% of the time
where the time goes in v7:
time: 32.6 us; the launch traced here: 32.5 us
  Pallas kernels  31.8 us (98%)
  between operations  0.64 us (2%)
    pallas_call x1, Pallas kernels, body(): pl.pallas_call(kernel, out_shape=[pltpu.VMEM(x.shape, BF16) for x in (que...  29.1 us
    pallas_call x1, Pallas kernels, body(): pl.pallas_call(store_kernel, out_shape=[jax.ShapeDtypeStruct(x.shape, BF1...  2.71 us

profile of v7, /device:TPU:0, one launch (start us, length us, event | category | flops | bytes accessed | tf_op | source)
XLA Modules:
  0.0 32.5 jit_solution(12502738373310520134)
XLA Ops:
  0.6 29.1 %packed_attention.1 = (bf16[256,5120]{1,0:T(8,128)(2,1)S(1)}, bf16[256,5120]{1,0:T(8,128)(2,1)S(1)}, bf16[256,1024]{1,0:T(8,128)(2,1)S(1)}, bf16[256,1024]{1,0:T(8,128)(2,1)S(1)}) custom-call(s32[16,64]{1,0:T(8,128)} %bitcast.1, bf16[256,5120]{1,0:T(8,128)(2,1)} %q_hbm.1, bf16[256,1024]{1,0:T(8,128)(2,1)} %k_hbm.1, bf16[256,1024]{1,0:T(8,128)(2,1)} %v_hbm.1, ...), custom_call_target="tpu_custom_call" | custom-call | tf_op jit(solution)/shard_map/packed_attention/pallas_call | solution.py:353
  29.8 2.7 %store_results.1 = (bf16[256,5120]{1,0:T(8,128)(2,1)}, bf16[256,5120]{1,0:T(8,128)(2,1)}, bf16[256,1024]{1,0:T(8,128)(2,1)}, bf16[256,1024]{1,0:T(8,128)(2,1)}) custom-call(bf16[256,5120]{1,0:T(8,128)(2,1)S(1)} %get-tuple-element.8.refs_0_, bf16[256,5120]{1,0:T(8,128)(2,1)S(1)} %get-tuple-element.9.refs_1_, bf16[256,1024]{1,0:T(8,128)(2,1)S(1)} %get-tuple-element.10.refs_2_, ...), custom_call_target="tpu_custom_call" | custom-call | tf_op jit(solution)/shard_map/store_results/pallas_call | solution.py:380

commit v8 on v7

--- a/solution.py
+++ b/solution.py
@@ -142,11 +142,10 @@
         every = kv_far.at[0:blocks]
         send(every, every, sent, 0).wait_send()
 
-    load(0).start()
-    load(1).start()
-
     @pl.when(head == 0)
     def _():
+        load(0).start()
+        load(1).start()
         pl.semaphore_wait(barrier, 1)
         load(0).wait()
         far(0, 0, 0).start()
@@ -243,9 +242,6 @@
 
     @pl.when(head == 1)
     def _():
-        load(4).start()
-        load(2).start()
-        load(3).start()
         pl.semaphore_wait(barrier, 1)
 
         @pl.when(core == 1)
@@ -253,6 +249,8 @@
             for i in range(4):
                 lend(i).start()
 
+        for i in (4, 2, 3, 0, 1):
+            load(i).start()
         load(4).wait()
         bias_a[...] = mask_bias(lengths, seq, ROWS, 0, ROWS + HALF)
         bias_b[...] = mask_bias(lengths, seq, ROWS + HALF, ROWS + HALF, HALF)

time: 32.6 us -> 32.6 us (level)
  no operation moved by 1% of the time
where the time goes in v8:
time: 32.6 us; the launch traced here: 32.5 us
  Pallas kernels  31.8 us (98%)
  between operations  0.64 us (2%)
    pallas_call x1, Pallas kernels, body(): pl.pallas_call(kernel, out_shape=[pltpu.VMEM(x.shape, BF16) for x in (que...  29.1 us
    pallas_call x1, Pallas kernels, body(): pl.pallas_call(store_kernel, out_shape=[jax.ShapeDtypeStruct(x.shape, BF1...  2.71 us

profile of v8, /device:TPU:0, one launch (start us, length us, event | category | flops | bytes accessed | tf_op | source)
XLA Modules:
  0.0 32.5 jit_solution(3368390162941974404)
XLA Ops:
  0.6 29.1 %packed_attention.1 = (bf16[256,5120]{1,0:T(8,128)(2,1)S(1)}, bf16[256,5120]{1,0:T(8,128)(2,1)S(1)}, bf16[256,1024]{1,0:T(8,128)(2,1)S(1)}, bf16[256,1024]{1,0:T(8,128)(2,1)S(1)}) custom-call(s32[16,64]{1,0:T(8,128)} %bitcast.1, bf16[256,5120]{1,0:T(8,128)(2,1)} %q_hbm.1, bf16[256,1024]{1,0:T(8,128)(2,1)} %k_hbm.1, bf16[256,1024]{1,0:T(8,128)(2,1)} %v_hbm.1, ...), custom_call_target="tpu_custom_call" | custom-call | tf_op jit(solution)/shard_map/packed_attention/pallas_call | solution.py:351
  29.8 2.7 %store_results.1 = (bf16[256,5120]{1,0:T(8,128)(2,1)}, bf16[256,5120]{1,0:T(8,128)(2,1)}, bf16[256,1024]{1,0:T(8,128)(2,1)}, bf16[256,1024]{1,0:T(8,128)(2,1)}) custom-call(bf16[256,5120]{1,0:T(8,128)(2,1)S(1)} %get-tuple-element.8.refs_0_, bf16[256,5120]{1,0:T(8,128)(2,1)S(1)} %get-tuple-element.9.refs_1_, bf16[256,1024]{1,0:T(8,128)(2,1)S(1)} %get-tuple-element.10.refs_2_, ...), custom_call_target="tpu_custom_call" | custom-call | tf_op jit(solution)/shard_map/store_results/pallas_call | solution.py:378
